TPU v7x, 32 devices: a whole 2x2x4 slice. The times are simulated.
32 devices in a mesh: grp: 2 (over y), wloop: 4 (over z), head: 4 (over x, core).
Axes of the slice: x: 2, y: 2, z: 4, core: 2. Of those that a mesh axis runs over, the one named last changes fastest.
Arguments:
- tokens: bfloat16 [4096, 8192], P(('grp', 'wloop'), 'head'), parts along dimension 0, may hold values from -200 to 200
- norm_gain: float32 [8192], replicated, may hold values from 0.1 to 1.9
- w_query: bfloat16 [8192, 8192], P('wloop', 'head'), may hold values from -0.0625 to 0.0625
- w_key: bfloat16 [8192, 1024], P('wloop', 'head'), may hold values from -0.0625 to 0.0625
- w_value: bfloat16 [8192, 1024], P('wloop', 'head'), may hold values from -0.0625 to 0.0625
- cache_key: bfloat16 [32, 1024, 1024], P(('grp', 'wloop'), None, 'head'), parts along dimension 0, may hold values from -600 to 600
- cache_value: bfloat16 [32, 1024, 1024], P(('grp', 'wloop'), None, 'head'), parts along dimension 0, may hold values from -6 to 6
- turn_len: int32 [32], P(('grp', 'wloop')), parts along dimension 0, may hold values from 1 to 128, as said below
- cache_len: int32 [32], P(('grp', 'wloop')), parts along dimension 0, may hold values from 1 to 1024, as said below
Outputs:
- attended: bfloat16 [4096, 8192], P(('grp', 'wloop'), 'head'), parts along dimension 0
- fresh_keys: bfloat16 [4096, 1024], P(('grp', 'wloop'), 'head'), parts along dimension 0
- fresh_values: bfloat16 [4096, 1024], P(('grp', 'wloop'), 'head'), parts along dimension 0
There are 2 independent parts, one for each index of `grp`. A program takes and returns all parts, laid end to end along the dimension named above; an argument that names none is the same for every part. Nothing has to cross between parts.
Inputs may be any that keep to these rules, and one draw needn't show every extreme that they name: Session s owns rows s * 128 to s * 128 + 127 of tokens; the first turn_len[s] of them are live, the rest padding. Slots 0 to cache_len[s] - 1 of session s's cache are filled, the others are padding; the new turn's positions follow the cached prefix.
All inputs are finite; a program needn't handle non-finite values.
Results may differ from a plain program's by a relative error of at most 0.012.
The roundings to bfloat16 on the way count: a program that leaves them out, or rounds other values in their place, can miss the bound.
Values may be sent and summed in bfloat16 or wider, within the bound.
A program may use at most 192 MiB of HBM per device.

v0:
```python
import jax
import jax.numpy as jnp
from jax import lax
from jax.sharding import PartitionSpec as P

HEAD_DIM = 128


EPSILON = 1e-06
THETA = 1000000.0


def rotate(vectors, positions):
    half_dim = vectors.shape[-1] // 2
    freq_index = jnp.arange(half_dim, dtype=jnp.float32)
    frequency = jnp.power(jnp.float32(THETA), freq_index * (-2.0 / vectors.shape[-1]))
    angles = positions[..., None] * frequency
    cosine = jnp.cos(angles)
    sine_part = jnp.sin(angles)
    lower_half = vectors[..., :half_dim]
    upper_half = vectors[..., half_dim:]
    return jnp.concatenate(
        [
            lower_half * cosine - upper_half * sine_part,
            upper_half * cosine + lower_half * sine_part,
        ],
        axis=-1,
    )


def project_rows(normed, weight_rows):
    return jnp.dot(normed, weight_rows, preferred_element_type=jnp.float32)


def attend_all(rotated, new_keys, new_values, old_keys, old_values, turn_len, cache_len):
    session_count, turn_size, kv_local, head_dim = new_keys.shape
    head_local = rotated.shape[2]
    group_size = head_local // kv_local
    cache_size = old_keys.shape[1]
    factor = head_dim ** (-0.5)
    grouped = rotated.reshape(session_count, turn_size, kv_local, group_size, head_dim)
    far_scores = (
        jnp.einsum("stkgd,slkd->skgtl", grouped, old_keys, preferred_element_type=jnp.float32)
        * factor
    )
    near_scores = (
        jnp.einsum("stkgd,sukd->skgtu", grouped, new_keys, preferred_element_type=jnp.float32)
        * factor
    )
    slot_index = jnp.arange(cache_size, dtype=jnp.int32)
    turn_index = jnp.arange(turn_size, dtype=jnp.int32)
    slot_live = slot_index[None, :] < cache_len[:, None]
    far_scores = jnp.where(slot_live[:, None, None, None, :], far_scores, -jnp.inf)
    near_scores = jnp.where(turn_index[None, :] <= turn_index[:, None], near_scores, -jnp.inf)
    row_max = jnp.maximum(jnp.max(far_scores, axis=-1), jnp.max(near_scores, axis=-1))[..., None]
    far_exp = jnp.exp(far_scores - row_max)
    near_exp = jnp.exp(near_scores - row_max)
    totals = jnp.sum(far_exp, axis=-1, keepdims=True) + jnp.sum(near_exp, axis=-1, keepdims=True)
    far_weights = (far_exp / totals).astype(jnp.bfloat16)
    near_weights = (near_exp / totals).astype(jnp.bfloat16)
    mixed = jnp.einsum(
        "skgtl,slkd->stkgd", far_weights, old_values, preferred_element_type=jnp.float32
    )
    mixed = mixed + jnp.einsum(
        "skgtu,sukd->stkgd", near_weights, new_values, preferred_element_type=jnp.float32
    )
    live_rows = turn_index[None, :] < turn_len[:, None]
    mixed = jnp.where(live_rows[:, :, None, None, None], mixed, 0.0)
    return mixed.reshape(session_count * turn_size, head_local * head_dim).astype(jnp.bfloat16)


def local(tokens, norm_gain, w_query, w_key, w_value, cache_key, cache_value, turn_len, cache_len):
    gathered = lax.all_gather(tokens, "head", axis=1, tiled=True)
    widened = gathered.astype(jnp.float32)
    inverse_rms = lax.rsqrt(jnp.mean(widened * widened, axis=1, keepdims=True) + EPSILON)
    normed = (widened * inverse_rms * norm_gain).astype(jnp.bfloat16)
    row_count = normed.shape[0]
    query_width = w_query.shape[1]
    pair_width = w_key.shape[1]
    queries = project_rows(normed, lax.all_gather(w_query, "wloop", axis=0, tiled=True))
    keys_raw = project_rows(normed, lax.all_gather(w_key, "wloop", axis=0, tiled=True))
    values_raw = project_rows(normed, lax.all_gather(w_value, "wloop", axis=0, tiled=True))
    session_count = turn_len.shape[0]
    turn_size = row_count // session_count
    head_local = query_width // HEAD_DIM
    kv_local = pair_width // HEAD_DIM
    turn_index = jnp.arange(turn_size, dtype=jnp.int32)
    positions = (cache_len[:, None] + turn_index[None, :]).astype(jnp.float32)[:, :, None]
    live_rows = turn_index[None, :] < turn_len[:, None]
    rotated = rotate(
        queries.reshape(session_count, turn_size, head_local, HEAD_DIM), positions
    ).astype(jnp.bfloat16)
    new_keys = jnp.where(
        live_rows[:, :, None, None],
        rotate(keys_raw.reshape(session_count, turn_size, kv_local, HEAD_DIM), positions),
        0.0,
    ).astype(jnp.bfloat16)
    new_values = jnp.where(
        live_rows[:, :, None, None],
        values_raw.reshape(session_count, turn_size, kv_local, HEAD_DIM),
        0.0,
    ).astype(jnp.bfloat16)
    old_keys = cache_key.reshape(session_count, cache_key.shape[1], kv_local, HEAD_DIM)
    old_values = cache_value.reshape(session_count, cache_value.shape[1], kv_local, HEAD_DIM)
    attended = attend_all(rotated, new_keys, new_values, old_keys, old_values, turn_len, cache_len)
    return (
        attended,
        new_keys.reshape(row_count, pair_width),
        new_values.reshape(row_count, pair_width),
    )


def solution(mesh):
    placed = (
        P(("grp", "wloop"), "head"),
        P(),
        P("wloop", "head"),
        P("wloop", "head"),
        P("wloop", "head"),
        P(("grp", "wloop"), None, "head"),
        P(("grp", "wloop"), None, "head"),
        P(("grp", "wloop")),
        P(("grp", "wloop")),
    )
    return jax.shard_map(
        local,
        mesh=mesh,
        in_specs=placed,
        out_specs=(
            P(("grp", "wloop"), "head"),
            P(("grp", "wloop"), "head"),
            P(("grp", "wloop"), "head"),
        ),
        check_vma=False,
    )
```

profile of v0, /device:TPU:8, one launch (start us, length us, event | category | flops | bytes accessed | tf_op | source)
XLA Modules:
  0.0 877.3 jit_solution(8610278054511559278)
XLA Ops:
  7.2 0.0 all-gather.5.cloned.1.call-start
  7.2 0.7 all-gather.5.cloned.1.call-update
  7.9 0.0 all-gather.9.cloned.1.call-start
  7.9 0.7 all-gather.9.cloned.1.call-update
  8.6 0.0 all-gather.11.cloned.1.call-start
  8.7 0.7 all-gather.11.cloned.1.call-update
  9.4 0.0 all-gather.7.cloned.1.call-start
  9.4 0.5 all-gather.7.cloned.1.call-update
  10.0 0.0 copy-done.2
  10.0 0.1 add_convert_fusion.1
  10.1 0.5 multiply_cosine_fusion
  10.7 0.1 copy.25
  10.8 0.1 copy.26
  10.9 0.1 copy-done
  11.0 2.0 reshape.151
  13.0 4.0 reshape.153
  17.0 0.1 fusion.33
  17.1 0.1 iota_compare_fusion.1
  17.2 51.9 %all-gather.5.cloned.1.call-done = bf16[512,8192]{1,0:T(8,128)(2,1)} async-done(((bf16[512,2048]{1,0:T(8,128)(2,1)}), bf16[512,8192]{1,0:T(8,128)(2,1)}) %all-gather.5.cloned.1.call-update) | async-done | bytes 8388624 | tf_op jit(solution)/shard_map/all_gather | solution.py:73
  69.1 5.1 fusion.2
  74.2 74.6 %all-gather.9.cloned.1.call-done = bf16[8192,256]{1,0:T(8,128)(2,1)} async-done(((bf16[2048,256]{1,0:T(8,128)(2,1)}), bf16[8192,256]{1,0:T(8,128)(2,1)}) %all-gather.9.cloned.1.call-update) | async-done | bytes 4194320 | tf_op jit(solution)/shard_map/all_gather | solution.py:81
  148.8 7.0 fusion.36
  155.7 0.3 reshape.152
  156.0 0.6 fusion.39
  156.6 0.2 copy.51
  156.8 0.2 copy.52
  157.0 0.1 multiply_subtract_fusion
  157.1 0.2 copy.38
  157.3 72.3 %all-gather.11.cloned.1.call-done = bf16[8192,256]{1,0:T(8,128)(2,1)} async-done(((bf16[2048,256]{1,0:T(8,128)(2,1)}), bf16[8192,256]{1,0:T(8,128)(2,1)}) %all-gather.11.cloned.1.call-update) | async-done | bytes 4194320 | tf_op jit(solution)/shard_map/all_gather | solution.py:82
  229.7 7.7 select_convert_fusion
  237.4 0.1 reshape.154
  237.4 0.2 copy.34
  237.6 553.1 %all-gather.7.cloned.1.call-done = bf16[8192,2048]{1,0:T(8,128)(2,1)} async-done(((bf16[2048,2048]{1,0:T(8,128)(2,1)}), bf16[8192,2048]{1,0:T(8,128)(2,1)}) %all-gather.7.cloned.1.call-update) | async-done | bytes 33554448 | tf_op jit(solution)/shard_map/all_gather | solution.py:80
  790.7 24.0 %convolution_bitcast_fusion = f32[64,8,16,128]{3,1,2,0:T(8,128)S(1)} fusion(bf16[8192,2048]{1,0:T(8,128)(2,1)} %all-gather.7.cloned.1.call-done, bf16[512,8192]{1,0:T(8,128)(2,1)} %all-gather.5.cloned.1.call-done, f32[8192]{0:T(1024)S(1)} %copy-done.3, f32[512]{0:T(512)S(1)} %add_rsqrt_fusion), kind=kOutput, calls=%fused_computation.22 | convolution fusion | flops 17196646400 | bytes 46172160 | tf_op jit(solution)/shard_map/dot_general | solution.py:32
  814.7 0.9 copy.53
  815.7 1.9 subtract_convert_fusion
  817.5 0.5 copy.27
  818.1 0.5 copy.28
  818.6 2.0 fusion.9
  820.6 15.1 %bitcast_reduce_fusion = (f32[4,2,8,128]{3,2,1,0:T(8,128)S(1)}, f32[4,2,128,8,1024]{4,2,3,1,0:T(8,128)}) fusion(pred[4,1024]{1,0:T(4,128)(4,1)S(1)} %iota_compare_fusion.1, bf16[4,1024,2,128,1]{3,2,1,0,4:T(2,128)(2,1)} %bitcast.67, bf16[4,128,2,8,64]{4,1,3,2,0:T(8,128)(2,1)S(1)} %bitcast.66, bf16[4,128,2,8,64]{4,1,3,2,0:T(8,128)(2,1)S(1)} %bitcast.64), kind=kOutput, calls=%fused_computation.1 | convolution fusion | flops 2176835584 | bytes 37785600 | tf_op jit(solution)/shard_map/stkgd,slkd->skgtl/dot_general | solution.py:43
  835.8 1.1 fusion.8
  836.9 14.6 %fusion.1 = f32[4,2,8,128]{3,2,1,0:T(8,128)S(1)} fusion(f32[4,2,128,8,1024]{4,2,3,1,0:T(8,128)} %get-tuple-element.16, f32[4,2,8,128]{3,2,1,0:T(8,128)S(1)} %max.7, pred[4,1024]{1,0:T(4,128)(4,1)S(1)} %iota_compare_fusion.1), kind=kLoop, calls=%fused_computation.5 | loop fusion | flops 33546240 | bytes 33624064 | tf_op jit(solution)/shard_map/reduce_sum | solution.py:58
  851.5 0.0 copy-start.1
  851.5 1.3 fusion.13
  852.8 0.3 copy-done.1
  853.1 14.0 %fusion.7 = bf16[4,128,2,8,128]{4,1,3,2,0:T(8,128)(2,1)S(1)} fusion(f32[4,2,128,8,128]{2,4,3,1,0:T(8,128)S(1)} %fusion.13, f32[4,2,128,8,1024]{4,2,3,1,0:T(8,128)} %get-tuple-element.16, f32[4,2,8,128]{3,2,1,0:T(8,128)S(1)} %add.49, f32[4,2,8,128]{3,2,1,0:T(8,128)S(1)} %max.7, pred[4,1024]{1,0:T(4,128)(4,1)S(1)} %iota_compare_fusion.1, ...), kind=kOutput, calls=%fused_computation.14 | convolution fusion | flops 2192572416 | bytes 42013184 | tf_op jit(solution)/shard_map/skgtl,slkd->stkgd/dot_general | solution.py:61
  867.2 1.4 copy.37
  868.5 2.3 convert_element_type.47
  (12 shorter events, 0.1 us)
Async XLA Ops:
  7.2 61.9 %all-gather.5.cloned.1.call-start = ((), (), s32[]{:S(2)}) async-start(), calls=%async_computation | async-start | bytes 10485760 | tf_op jit(solution)/shard_map/all_gather | solution.py:73
  7.9 140.9 %all-gather.9.cloned.1.call-start = ((), (), s32[]{:S(2)}) async-start(), calls=%async_computation.2 | async-start | bytes 5242880 | tf_op jit(solution)/shard_map/all_gather | solution.py:81
  8.6 221.0 %all-gather.11.cloned.1.call-start = ((), (), s32[]{:S(2)}) async-start(), calls=%async_computation.3 | async-start | bytes 5242880 | tf_op jit(solution)/shard_map/all_gather | solution.py:82
  9.4 0.7 copy-start.2
  9.4 1.6 copy-start
  9.4 781.3 %all-gather.7.cloned.1.call-start = ((), (), s32[]{:S(2)}) async-start(), calls=%async_computation.1 | async-start | bytes 41943040 | tf_op jit(solution)/shard_map/all_gather | solution.py:80
  11.0 6.0 copy-start.4
  17.2 131.6 %copy-start.3 = (f32[8192]{0:T(1024)S(1)}, f32[8192]{0:T(1024)}, u32[]{:S(2)}) copy-start(f32[8192]{0:T(1024)} %param.10) | copy-start | bytes 98308
  851.5 1.6 copy-start.1
Sparse Core Ops, SparseCore 0:
  9.6 59.4 all-gather.4
  70.6 78.0 all-gather.8
  150.3 79.2 all-gather.10
  231.1 559.5 all-gather.6
where the time goes:
time: 882 us; the launch traced here: 877 us
  waiting for transfers between devices  754 us (85%)
  matrix products  71.1 us (8%)
  other arithmetic  23.6 us (3%)
  local copies, waits for them, and re-layouts  14 us (2%)
  between operations  14 us (2%)
    all_gather x1, waiting for transfers between devices, local(): lax.all_gather(w_query, 'wloop', axis=0, tiled=True)  553 us
    all_gather x1, waiting for transfers between devices, local(): lax.all_gather(w_key, 'wloop', axis=0, tiled=True)  74.6 us
    all_gather x1, waiting for transfers between devices, local(): lax.all_gather(w_value, 'wloop', axis=0, tiled=True)  72.3 us
    all_gather x1, waiting for transfers between devices, local(): gathered = lax.all_gather(tokens, 'head', axis=1, tiled=True)  51.9 us
    dot_general x3, matrix products, project_rows(): return jnp.dot(normed, weight_rows, preferred_element_type=jnp.float32)  38.7 us
  transfers between devices with their start and end apart: 4, of which 4 were waited for; matrix products, arithmetic and copies ran while one was open for 3% of the time, Pallas kernels for 0%

commit v1 on v0

--- a/solution.py
+++ b/solution.py
@@ -69,7 +69,7 @@
     return mixed.reshape(session_count * turn_size, head_local * head_dim).astype(jnp.bfloat16)
 
 
-def local(tokens, norm_gain, w_query, w_key, w_value, cache_key, cache_value, turn_len, cache_len):
+def local_gather(tokens, norm_gain, w_query, w_key, w_value, cache_key, cache_value, turn_len, cache_len):
     gathered = lax.all_gather(tokens, "head", axis=1, tiled=True)
     widened = gathered.astype(jnp.float32)
     inverse_rms = lax.rsqrt(jnp.mean(widened * widened, axis=1, keepdims=True) + EPSILON)
@@ -110,6 +110,129 @@
     )
 
 
+def transposed_tokens(tokens, ways):
+    row_count = tokens.shape[0]
+    session_rows = row_count // ways
+    w_at = lax.axis_index("wloop")
+    h_at = lax.axis_index("head")
+    received = []
+    for shift in range(ways):
+        target = lax.rem(w_at + shift, ways)
+        piece = lax.dynamic_slice_in_dim(tokens, target * session_rows, session_rows, 0)
+        pairs = [
+            (w * ways + h, h * ways + (w + shift) % ways) for w in range(ways) for h in range(ways)
+        ]
+        received.append(lax.ppermute(piece, ("wloop", "head"), pairs))
+    stacked = jnp.stack(received)
+    order = lax.rem(h_at + ways - jnp.arange(ways), ways)
+    own_rows = jnp.take(stacked, order, axis=0)
+    return lax.all_gather(own_rows, "head", axis=0)
+
+
+def reduce_over_line(partials, ways):
+    w_at = lax.axis_index("wloop")
+
+    def pick(index):
+        return lax.dynamic_index_in_dim(
+            partials, jnp.clip(index, 0, ways - 1), 0, keepdims=False
+        )
+
+    rising = None
+    falling = None
+    for step in range(1, ways):
+        up = pick(w_at + ways - step)
+        down = pick(w_at - ways + step)
+        if rising is not None:
+            up = up + rising.astype(jnp.float32)
+            down = down + falling.astype(jnp.float32)
+        rising = lax.ppermute(
+            up.astype(jnp.bfloat16), "wloop", [(w, w + 1) for w in range(step)]
+        )
+        falling = lax.ppermute(
+            down.astype(jnp.bfloat16), "wloop", [(ways - 1 - w, ways - 2 - w) for w in range(step)]
+        )
+    return pick(w_at) + rising.astype(jnp.float32) + falling.astype(jnp.float32)
+
+
+def local_reduce(
+    tokens, norm_gain, w_query, w_key, w_value, cache_key, cache_value, turn_len, cache_len
+):
+    ways = lax.axis_size("wloop")
+    row_count = tokens.shape[0]
+    depth = w_query.shape[0]
+    width = norm_gain.shape[0]
+    kv_local = w_key.shape[1] // HEAD_DIM
+    head_local = w_query.shape[1] // HEAD_DIM
+    group_size = head_local // kv_local
+    session_count = turn_len.shape[0]
+    turn_size = row_count // session_count
+    cache_size = cache_key.shape[1]
+    w_at = lax.axis_index("wloop")
+
+    widened = tokens.astype(jnp.float32)
+    squares = jnp.sum(widened * widened, axis=1)
+    all_squares = lax.all_gather(squares, ("wloop", "head"), axis=0)
+    mean = jnp.sum(all_squares.reshape(ways, ways, row_count), axis=1) / width
+    inverse_rms = lax.rsqrt(mean + EPSILON).reshape(ways, ways, row_count // ways)
+    inverse_rms = jnp.transpose(inverse_rms, (1, 0, 2))
+
+    gathered = transposed_tokens(tokens, ways)
+    gain = lax.dynamic_slice_in_dim(norm_gain, w_at * depth, depth, 0)
+    normed = (gathered.astype(jnp.float32) * inverse_rms[..., None] * gain).astype(jnp.bfloat16)
+    normed = jnp.transpose(normed, (1, 0, 2, 3)).reshape(ways, row_count, depth)
+
+    turn_index = jnp.arange(turn_size, dtype=jnp.int32)
+    positions = (cache_len[:, None] + turn_index[None, :]).astype(jnp.float32)[:, :, None]
+    live_rows = turn_index[None, :] < turn_len[:, None]
+    outs = []
+    for kv in range(kv_local):
+        q_cols = group_size * HEAD_DIM
+        weights = jnp.concatenate(
+            [
+                w_query[:, kv * q_cols : (kv + 1) * q_cols],
+                w_key[:, kv * HEAD_DIM : (kv + 1) * HEAD_DIM],
+                w_value[:, kv * HEAD_DIM : (kv + 1) * HEAD_DIM],
+            ],
+            axis=1,
+        )
+        partials = jnp.einsum("brd,dn->brn", normed, weights, preferred_element_type=jnp.float32)
+        summed = reduce_over_line(partials, ways)
+        queries = summed[:, :q_cols]
+        keys_raw = summed[:, q_cols : q_cols + HEAD_DIM]
+        values_raw = summed[:, q_cols + HEAD_DIM :]
+        rotated = rotate(
+            queries.reshape(session_count, turn_size, group_size, HEAD_DIM), positions
+        ).astype(jnp.bfloat16)
+        new_keys = jnp.where(
+            live_rows[:, :, None, None],
+            rotate(keys_raw.reshape(session_count, turn_size, 1, HEAD_DIM), positions),
+            0.0,
+        ).astype(jnp.bfloat16)
+        new_values = jnp.where(
+            live_rows[:, :, None, None],
+            values_raw.reshape(session_count, turn_size, 1, HEAD_DIM),
+            0.0,
+        ).astype(jnp.bfloat16)
+        old_keys = cache_key[:, :, kv * HEAD_DIM : (kv + 1) * HEAD_DIM][:, :, None, :]
+        old_values = cache_value[:, :, kv * HEAD_DIM : (kv + 1) * HEAD_DIM][:, :, None, :]
+        attended = attend_all(
+            rotated, new_keys, new_values, old_keys, old_values, turn_len, cache_len
+        )
+        outs.append(
+            (attended, new_keys.reshape(row_count, -1), new_values.reshape(row_count, -1))
+        )
+    return tuple(jnp.concatenate(arrays, axis=1) for arrays in zip(*outs))
+
+
+def local(*args):
+    tokens, norm_gain = args[0], args[1]
+    w_ways, h_ways = lax.axis_size("wloop"), lax.axis_size("head")
+    if w_ways == h_ways and w_ways > 1 and tokens.shape[0] % w_ways == 0:
+        if w_ways * tokens.shape[0] < norm_gain.shape[0]:
+            return local_reduce(*args)
+    return local_gather(*args)
+
+
 def solution(mesh):
     placed = (
         P(("grp", "wloop"), "head"),

time: 882 us -> 488 us (0.55)
  waiting for transfers between devices: 754 us -> 238 us
  blocking collectives: 0 us -> 38.2 us
  starting transfers between devices: 0.15 us -> 32.2 us
  other arithmetic: 23.6 us -> 52.9 us
  local copies, waits for them, and re-layouts: 14 us -> 39.8 us
    all_gather x4 -> x1, waiting for transfers between devices: 752 us -> 32.4 us  [transposed_tokens(): return lax.all_gather(own_rows, 'head', axis=0)]
    ppermute x0 -> x16, waiting for transfers between devices: none -> 206 us  [the longest x6 73.7 us: reduce_over_line(): lax.ppermute(up.astype(jnp.bfloat16), 'wloop', [(w, w + 1) for w in range...]
    all_gather x0 -> x1, blocking collectives: none -> 38.2 us  [local_reduce(): all_squares = lax.all_gather(squares, ('wloop', 'head'), axis=0)]
    ppermute x0 -> x16, starting transfers between devices: none -> 32.2 us  [the longest x6 15.4 us: reduce_over_line(): lax.ppermute(up.astype(jnp.bfloat16), 'wloop', [(w, w + 1) for w in range...]
    convert_element_type x1 -> x9, other arithmetic: 0.07 us -> 31 us  [the longest x4 16 us: reduce_over_line(): up.astype(jnp.bfloat16)]
    unnamed x13 -> x68, local copies, waits for them, and re-layouts: 1.72 us -> 18.1 us
    dot_general x3 -> x2, matrix products: 38.7 us -> 25.9 us  [local_reduce(): jnp.einsum('brd,dn->brn', normed, weights, preferred_element_type=jnp.flo...]
    slice x0 -> x8, local copies, waits for them, and re-layouts: none -> 12 us  [the longest x1 6.09 us: local_reduce(): w_query[:, kv * q_cols:(kv + 1) * q_cols]]
  transfers between devices with their start and end apart: 4 -> 17, of which waited for: 4 -> 11; matrix products, arithmetic and copies ran while one was open for 3% -> 10% of each run, Pallas kernels for 0% -> 0%
where the time goes in v1:
time: 488 us; the launch traced here: 480 us
  waiting for transfers between devices  238 us (49%)
  matrix products  63.8 us (13%)
  other arithmetic  52.9 us (11%)
  local copies, waits for them, and re-layouts  39.8 us (8%)
  blocking collectives  38.2 us (8%)
  starting transfers between devices  32.2 us (7%)
  between operations  15 us (3%)
    ppermute x6, waiting for transfers between devices, reduce_over_line(): lax.ppermute(up.astype(jnp.bfloat16), 'wloop', [(w, w + 1) for w in range...  73.7 us
    ppermute x4, waiting for transfers between devices, transposed_tokens(): received.append(lax.ppermute(piece, ('wloop', 'head'), pairs))  66.2 us
    ppermute x6, waiting for transfers between devices, reduce_over_line(): lax.ppermute(down.astype(jnp.bfloat16), 'wloop', [(ways - 1 - w, ways - 2...  66 us
    all_gather x1, blocking collectives, local_reduce(): all_squares = lax.all_gather(squares, ('wloop', 'head'), axis=0)  38.2 us
    all_gather x1, waiting for transfers between devices, transposed_tokens(): return lax.all_gather(own_rows, 'head', axis=0)  32.4 us
    dot_general x2, matrix products, local_reduce(): jnp.einsum('brd,dn->brn', normed, weights, preferred_element_type=jnp.flo...  25.9 us
    dot_general x2, matrix products, attend_all(): jnp.einsum('stkgd,slkd->skgtl', grouped, old_keys, preferred_element_type...  21.7 us
    unnamed x68, local copies, waits for them, and re-layouts  18.1 us
  transfers between devices with their start and end apart: 17, of which 11 were waited for; matrix products, arithmetic and copies ran while one was open for 10% of the time, Pallas kernels for 0%

profile of v1, /device:TPU:8, one launch (start us, length us, event | category | flops | bytes accessed | tf_op | source)
XLA Modules:
  0.0 480.3 jit_solution(7798446109460265083)
XLA Ops:
  8.9 1.9 collective-permute-start
  10.8 4.7 collective-permute-start.2
  15.6 4.8 collective-permute-done
  20.4 61.4 %collective-permute-done.2 = bf16[128,2048]{1,0:T(8,128)(2,1)S(1)} collective-permute-done((bf16[128,2048]{1,0:T(8,128)(2,1)S(1)}, bf16[128,2048]{1,0:T(8,128)(2,1)S(1)}, u32[]{:S(2)}, u32[]{:S(2)}) %collective-permute-start.2) | collective-permute-done | bytes 524320 | tf_op jit(solution)/shard_map/ppermute | solution.py:125
  83.2 2.0 gather_fusion
  85.2 3.2 bitcast_select_fusion.6
  90.5 38.2 %all-gather.1 = f32[16,1,512]{2,1,0:T(1,128)S(1)} all-gather(f32[1,1,512]{2,1,0:T(1,128)S(1)} %bitcast.300), channel_id=2, replica_groups=mesh['grp'=2,'wloop'=4,'head'=4] {'wloop','head'}, dimensions={0}, use_global_device_ids=true | all-gather | bytes 34816 | tf_op jit(solution)/shard_map/all_gather | solution.py:174
  128.9 2.6 fusion.119
  131.5 6.1 %fusion.116 = (bf16[2048,1024]{1,0:T(8,128)(2,1)}, bf16[2048,1024]{1,0:T(8,128)(2,1)}) fusion(bf16[2048,2048]{1,0:T(8,128)(2,1)} %param.11), kind=kLoop, calls=%fused_computation.184 | loop fusion | bytes 16777216 | tf_op jit(solution)/shard_map/slice | solution.py:192
  137.6 32.4 %all-gather.4.cloned.1.call-done = bf16[4,4,128,2048]{3,2,0,1:T(8,128)(2,1)} async-done(((bf16[1,4,128,2048]{3,2,0,1:T(8,128)(2,1)}), bf16[4,4,128,2048]{3,2,0,1:T(8,128)(2,1)}) %all-gather.4.cloned.1.call-update) | async-done | bytes 8388624 | tf_op jit(solution)/shard_map/all_gather | solution.py:129
  170.0 8.8 %multiply_convert_fusion = bf16[4,4,128,2048]{3,2,0,1:T(8,128)(2,1)} fusion(bf16[4,4,128,2048]{3,2,0,1:T(8,128)(2,1)} %all-gather.4.cloned.1.call-done, f32[2048]{0:T(1024)S(1)} %dynamic-slice-done, f32[4,4,128]{2,0,1:T(4,128)S(1)} %bitcast.299), kind=kLoop, calls=%fused_computation.9 | loop fusion | flops 16777216 | bytes 16793600 | tf_op jit(solution)/shard_map/convert_element_type | solution.py:181
  178.9 13.8 %fusion.15 = f32[4,512,1280]{2,1,0:T(8,128)S(1)} fusion(bf16[4,512,2048]{2,1,0:T(8,128)(2,1)} %bitcast.281, bf16[2048,128]{1,0:T(8,128)(2,1)} %get-tuple-element.62, bf16[2048,128]{1,0:T(8,128)(2,1)S(1)} %copy-done.19, bf16[2048,1024]{1,0:T(8,128)(2,1)S(1)} %copy-done.10), kind=kOutput, calls=%fused_computation.25 | convolution fusion | flops 10753146880 | bytes 24117248 | tf_op jit(solution)/shard_map/brd,dn->brn/dot_general | solution.py:198
  194.1 1.7 collective-permute-start.10
  195.9 2.4 copy-done.1
  198.5 12.1 %fusion.10 = f32[4,512,1280]{2,1,0:T(8,128)S(1)} fusion(bf16[4,512,2048]{2,1,0:T(8,128)(2,1)S(1)} %bitcast.282, bf16[2048,128]{1,0:T(8,128)(2,1)} %get-tuple-element.63, bf16[2048,128]{1,0:T(8,128)(2,1)S(1)} %copy-done.18, bf16[2048,1024]{1,0:T(8,128)(2,1)S(1)} %copy-done.9), kind=kOutput, calls=%fused_computation.19 | convolution fusion | flops 10753146880 | bytes 24117248 | tf_op jit(solution)/shard_map/brd,dn->brn/dot_general | solution.py:198
  210.6 3.8 copy-done
  217.1 1.8 collective-permute-start.13
  218.8 9.5 %collective-permute-done.10 = bf16[512,1280]{1,0:T(8,128)(2,1)} collective-permute-done((bf16[512,1280]{1,0:T(8,128)(2,1)}, bf16[512,1280]{1,0:T(8,128)(2,1)}, u32[]{:S(2)}, u32[]{:S(2)}) %collective-permute-start.10) | collective-permute-done | bytes 1310752 | tf_op jit(solution)/shard_map/ppermute | solution.py:148
  228.3 3.5 fusion.22
  231.8 1.9 collective-permute-start.11
  233.7 1.7 collective-permute-start.7
  235.5 21.0 %collective-permute-done.4 = bf16[512,1280]{1,0:T(8,128)(2,1)} collective-permute-done((bf16[512,1280]{1,0:T(8,128)(2,1)}, bf16[512,1280]{1,0:T(8,128)(2,1)}, u32[]{:S(2)}, u32[]{:S(2)}) %collective-permute-start.4) | collective-permute-done | bytes 1310752 | tf_op jit(solution)/shard_map/ppermute | solution.py:148
  256.4 3.5 fusion.27
  259.9 1.9 collective-permute-start.5
  261.8 22.7 %collective-permute-done.11 = bf16[512,1280]{1,0:T(8,128)(2,1)} collective-permute-done((bf16[512,1280]{1,0:T(8,128)(2,1)}, bf16[512,1280]{1,0:T(8,128)(2,1)}, u32[]{:S(2)}, u32[]{:S(2)}) %collective-permute-start.11) | collective-permute-done | bytes 1310752 | tf_op jit(solution)/shard_map/ppermute | solution.py:148
  284.5 5.3 %fusion.23 = (bf16[512,1280]{1,0:T(8,128)(2,1)}, bf16[512,1280]{1,0:T(8,128)(2,1)}) fusion(bf16[512,1280]{1,0:T(8,128)(2,1)} %collective-permute-done.11, f32[4,512,1280]{2,1,0:T(8,128)} %copy-done.1, s32[]{:T(128)S(6)} %min.30, bf16[512,1280]{1,0:T(8,128)(2,1)} %collective-permute-done.13, s32[]{:T(128)S(6)} %min.34), kind=kLoop, calls=%fused_computation.38 | loop fusion | flops 3932160 | bytes 10485768 | tf_op jit(solution)/shard_map/convert_element_type | solution.py:149
  291.4 20.6 %collective-permute-done.5 = bf16[512,1280]{1,0:T(8,128)(2,1)} collective-permute-done((bf16[512,1280]{1,0:T(8,128)(2,1)}, bf16[512,1280]{1,0:T(8,128)(2,1)}, u32[]{:S(2)}, u32[]{:S(2)}) %collective-permute-start.5) | collective-permute-done | bytes 1310752 | tf_op jit(solution)/shard_map/ppermute | solution.py:148
  311.9 3.8 fusion.28
  317.7 4.7 collective-permute-start.12
  323.0 2.0 fusion.21
  325.0 1.9 collective-permute-start.15
  327.6 3.9 collective-permute-start.6
  331.5 19.6 %collective-permute-done.8 = bf16[512,1280]{1,0:T(8,128)(2,1)S(1)} collective-permute-done((bf16[512,1280]{1,0:T(8,128)(2,1)S(1)}, bf16[512,1280]{1,0:T(8,128)(2,1)S(1)}, u32[]{:S(2)}, u32[]{:S(2)}) %collective-permute-start.8) | collective-permute-done | bytes 1310752 | tf_op jit(solution)/shard_map/ppermute | solution.py:151
  351.1 2.1 fusion.26
  353.1 1.9 collective-permute-start.9
  356.1 23.1 %collective-permute-done.15 = bf16[512,1280]{1,0:T(8,128)(2,1)S(1)} collective-permute-done((bf16[512,1280]{1,0:T(8,128)(2,1)S(1)}, bf16[512,1280]{1,0:T(8,128)(2,1)S(1)}, u32[]{:S(2)}, u32[]{:S(2)}) %collective-permute-start.15) | collective-permute-done | bytes 1310752 | tf_op jit(solution)/shard_map/ppermute | solution.py:151
  379.2 2.2 fusion.24
  382.8 22.8 %collective-permute-done.9 = bf16[512,1280]{1,0:T(8,128)(2,1)S(1)} collective-permute-done((bf16[512,1280]{1,0:T(8,128)(2,1)S(1)}, bf16[512,1280]{1,0:T(8,128)(2,1)S(1)}, u32[]{:S(2)}, u32[]{:S(2)}) %collective-permute-start.9) | collective-permute-done | bytes 1310752 | tf_op jit(solution)/shard_map/ppermute | solution.py:151
  405.6 2.2 fusion.29
  410.8 2.6 fusion.118
  415.0 2.2 copy.101
  417.4 2.0 select_convert_fusion.1
  422.8 1.9 subtract_convert_fusion.1
  424.7 7.6 %fusion.4 = (f32[4,8,128]{2,1,0:T(8,128)S(1)}, f32[4,128,8,1024]{3,1,2,0:T(8,128)}) fusion(pred[4,1024]{1,0:T(4,128)(4,1)S(1)} %iota_compare_fusion.1, bf16[4,1024,256]{2,1,0:T(8,128)(2,1)S(1)} %copy-done.13, bf16[4,128,8,64]{3,1,2,0:T(8,128)(2,1)S(1)} %get-tuple-element.16, bf16[4,128,8,64]{3,1,2,0:T(8,128)(2,1)S(1)} %get-tuple-element.15), kind=kOutput, calls=%fused_computation.12 | convolution fusion | flops 1088417792 | bytes 19943424 | tf_op jit(solution)/shard_map/stkgd,slkd->skgtl/dot_general | solution.py:43
  433.5 14.1 %fusion.2 = (f32[4,8,128]{2,1,0:T(8,128)S(1)}, f32[4,8,128]{2,1,0:T(8,128)S(1)}, f32[4,128,8,1024]{3,1,2,0:T(8,128)}) fusion(f32[4,128,8,1024]{3,1,2,0:T(8,128)} %get-tuple-element.56, f32[4,8,128]{2,1,0:T(8,128)S(1)} %max.54, pred[4,1024]{1,0:T(4,128)(4,1)S(1)} %iota_compare_fusion.1, bf16[4,1024,256]{2,1,0:T(8,128)(2,1)S(1)} %copy-done.13, ...), kind=kOutput, calls=%fused_computation.10 | convolution fusion | flops 1105190912 | bytes 36753408 | tf_op jit(solution)/shard_map/stkgd,slkd->skgtl/dot_general | solution.py:43
  449.3 8.3 %fusion.38 = bf16[4,128,1,8,128]{4,1,3,0,2:T(8,128)(2,1)S(1)} fusion(f32[4,128,8,128]{1,3,2,0:T(8,128)S(1)} %fusion.56, f32[4,8,128]{2,1,0:T(8,128)S(1)} %add.218, f32[4,8,128]{2,1,0:T(8,128)S(1)} %max.54, f32[4,128,8,1024]{3,1,2,0:T(8,128)} %get-tuple-element.56, pred[4,1024]{1,0:T(4,128)(4,1)S(1)} %iota_compare_fusion.1, ...), kind=kOutput, calls=%fused_computation.78 | convolution fusion | flops 1096286208 | bytes 21008896 | tf_op jit(solution)/shard_map/skgtl,slkd->stkgd/dot_general | solution.py:61
  459.9 3.9 fusion.3
  464.4 4.8 %fusion.41 = bf16[4,128,1,8,128]{4,1,3,0,2:T(8,128)(2,1)S(1)} fusion(f32[4,128,8,128]{1,3,2,0:T(8,128)S(1)} %fusion.54, f32[4,8,128]{2,1,0:T(8,128)S(1)} %add.229, f32[4,8,128]{2,1,0:T(8,128)S(1)} %max.55, f32[4,128,8,1024]{3,1,2,0:T(8,128)S(1)} %bitcast.278, pred[4,1024]{1,0:T(4,128)(4,1)S(1)} %iota_compare_fusion.1, ...), kind=kOutput, calls=%fused_computation.79 | convolution fusion | flops 1096286208 | bytes 21008896 | tf_op jit(solution)/shard_map/skgtl,slkd->stkgd/dot_general | solution.py:61
  (130 shorter events, 34.6 us)
Async XLA Ops:
  7.2 162.9 %all-gather.4.cloned.1.call-start = ((), (), s32[]{:S(2)}) async-start(), calls=%async_computation | async-start | bytes 10485760 | tf_op jit(solution)/shard_map/all_gather | solution.py:129
  8.9 11.4 %collective-permute-start = (bf16[128,2048]{1,0:T(8,128)(2,1)S(1)}, bf16[128,2048]{1,0:T(8,128)(2,1)S(1)}, u32[]{:S(2)}, u32[]{:S(2)}) collective-permute-start(bf16[128,2048]{1,0:T(8,128)(2,1)S(1)} %get-tuple-element.27), channel_id=1, source_target_pairs={{0,0},{1,4},{2,8},{3,12},{4,1},{5,5},{6,9},{7,13},{8,2},{9,6},{10,... | collective-permute-start | bytes 1572872 | tf_op jit(solution)/shard_map/ppermute | solution.py:125
  10.8 70.9 %collective-permute-start.2 = (bf16[128,2048]{1,0:T(8,128)(2,1)S(1)}, bf16[128,2048]{1,0:T(8,128)(2,1)S(1)}, u32[]{:S(2)}, u32[]{:S(2)}) collective-permute-start(bf16[128,2048]{1,0:T(8,128)(2,1)S(1)} %get-tuple-element.28), channel_id=1, source_target_pairs={{0,2},{1,6},{2,10},{3,14},{4,3},{5,7},{6,11},{7,15},{8,0},{9,4},{1... | collective-permute-start | bytes 1572872 | tf_op jit(solution)/shard_map/ppermute | solution.py:125
  15.5 66.2 %collective-permute-start.1 = (bf16[128,2048]{1,0:T(8,128)(2,1)S(1)}, bf16[128,2048]{1,0:T(8,128)(2,1)}, u32[]{:S(2)}, u32[]{:S(2)}) collective-permute-start(bf16[128,2048]{1,0:T(8,128)(2,1)S(1)} %get-tuple-element.29), channel_id=1, source_target_pairs={{0,1},{1,5},{2,9},{3,13},{4,2},{5,6},{6,10},{7,14},{8,3},{9,7},{10... | collective-permute-start | bytes 1572872 | tf_op jit(solution)/shard_map/ppermute | solution.py:125
  15.5 66.2 %collective-permute-start.3 = (bf16[128,2048]{1,0:T(8,128)(2,1)S(1)}, bf16[128,2048]{1,0:T(8,128)(2,1)}, u32[]{:S(2)}, u32[]{:S(2)}) collective-permute-start(bf16[128,2048]{1,0:T(8,128)(2,1)S(1)} %get-tuple-element.30), channel_id=1, source_target_pairs={{0,3},{1,7},{2,11},{3,15},{4,0},{5,4},{6,8},{7,12},{8,1},{9,5},{10... | collective-permute-start | bytes 1572872 | tf_op jit(solution)/shard_map/ppermute | solution.py:125
  88.4 1.6 copy-start.6
  88.4 40.5 %copy-start.12 = (bf16[2048,256]{1,0:T(8,128)(2,1)S(1)}, bf16[2048,256]{1,0:T(8,128)(2,1)}, u32[]{:S(2)}) copy-start(bf16[2048,256]{1,0:T(8,128)(2,1)} %param.12) | copy-start | bytes 3145732
  131.5 38.5 %dynamic-slice-start = ((f32[8192]{0:T(1024)}, s32[]{:T(128)}), f32[2048]{0:T(1024)S(1)}, s32[]{:S(2)}) async-start(f32[8192]{0:T(1024)} %param.10, s32[]{:T(128)} %select_n.130), calls=%async_computation.7 | async-start | bytes 16896 | tf_op jit(solution)/shard_map/dynamic_slice | solution.py:180
  170.0 8.8 %copy-start.10 = (bf16[2048,1024]{1,0:T(8,128)(2,1)S(1)}, bf16[2048,1024]{1,0:T(8,128)(2,1)}, u32[]{:S(2)}) copy-start(bf16[2048,1024]{1,0:T(8,128)(2,1)} %get-tuple-element.14) | copy-start | bytes 12582916
  170.0 8.8 %copy-start.19 = (bf16[2048,128]{1,0:T(8,128)(2,1)S(1)}, bf16[2048,128]{1,0:T(8,128)(2,1)}, u32[]{:S(2)}) copy-start(bf16[2048,128]{1,0:T(8,128)(2,1)} %get-tuple-element.32) | copy-start | bytes 1572868
  178.9 19.4 %copy-start.5 = (bf16[4,4,128,2048]{3,2,0,1:T(8,128)(2,1)S(1)}, bf16[4,4,128,2048]{3,2,0,1:T(8,128)(2,1)}, u32[]{:S(2)}) copy-start(bf16[4,4,128,2048]{3,2,0,1:T(8,128)(2,1)} %multiply_convert_fusion) | copy-start | bytes 25165828
  192.7 5.6 %copy-start.1 = (f32[4,512,1280]{2,1,0:T(8,128)}, f32[4,512,1280]{2,1,0:T(8,128)S(1)}, u32[]{:S(2)}) copy-start(f32[4,512,1280]{2,1,0:T(8,128)S(1)} %fusion.15) | copy-start | bytes 31457284
  192.7 5.6 %copy-start.9 = (bf16[2048,1024]{1,0:T(8,128)(2,1)S(1)}, bf16[2048,1024]{1,0:T(8,128)(2,1)}, u32[]{:S(2)}) copy-start(bf16[2048,1024]{1,0:T(8,128)(2,1)} %get-tuple-element.13) | copy-start | bytes 12582916
  192.7 5.8 %copy-start.18 = (bf16[2048,128]{1,0:T(8,128)(2,1)S(1)}, bf16[2048,128]{1,0:T(8,128)(2,1)}, u32[]{:S(2)}) copy-start(bf16[2048,128]{1,0:T(8,128)(2,1)} %get-tuple-element.31) | copy-start | bytes 1572868
  194.1 34.2 %collective-permute-start.10 = (bf16[512,1280]{1,0:T(8,128)(2,1)}, bf16[512,1280]{1,0:T(8,128)(2,1)}, u32[]{:S(2)}, u32[]{:S(2)}) collective-permute-start(bf16[512,1280]{1,0:T(8,128)(2,1)} %get-tuple-element.11), channel_id=1, source_target_pairs={{0,4},{1,5},{2,6},{3,7},{16,20},{17,21},{18,22},{19,23}} | collective-permute-start | bytes 3932168 | tf_op jit(solution)/shard_map/ppermute | solution.py:148
  210.6 3.8 copy-start
  215.8 40.6 %collective-permute-start.4 = (bf16[512,1280]{1,0:T(8,128)(2,1)}, bf16[512,1280]{1,0:T(8,128)(2,1)}, u32[]{:S(2)}, u32[]{:S(2)}) collective-permute-start(bf16[512,1280]{1,0:T(8,128)(2,1)} %get-tuple-element.7), channel_id=1, source_target_pairs={{0,4},{1,5},{2,6},{3,7},{16,20},{17,21},{18,22},{19,23}} | collective-permute-start | bytes 3932168 | tf_op jit(solution)/shard_map/ppermute | solution.py:148
  217.1 44.7 %collective-permute-start.13 = (bf16[512,1280]{1,0:T(8,128)(2,1)S(1)}, bf16[512,1280]{1,0:T(8,128)(2,1)}, u32[]{:S(2)}, u32[]{:S(2)}) collective-permute-start(bf16[512,1280]{1,0:T(8,128)(2,1)S(1)} %get-tuple-element.12), channel_id=1, source_target_pairs={{12,8},{13,9},{14,10},{15,11},{28,24},{29,25},{30,26},{31,27}} | collective-permute-start | bytes 3932168 | tf_op jit(solution)/shard_map/ppermute | solution.py:151
  231.8 52.7 %collective-permute-start.11 = (bf16[512,1280]{1,0:T(8,128)(2,1)}, bf16[512,1280]{1,0:T(8,128)(2,1)}, u32[]{:S(2)}, u32[]{:S(2)}) collective-permute-start(bf16[512,1280]{1,0:T(8,128)(2,1)} %fusion.22), channel_id=1, source_target_pairs={{0,4},{4,8},{1,5},{5,9},{2,6},{6,10},{3,7},{7,11},{16,20},{20,24},... | collective-permute-start | bytes 3932168 | tf_op jit(solution)/shard_map/ppermute | solution.py:148
  233.7 57.6 %collective-permute-start.7 = (bf16[512,1280]{1,0:T(8,128)(2,1)S(1)}, bf16[512,1280]{1,0:T(8,128)(2,1)}, u32[]{:S(2)}, u32[]{:S(2)}) collective-permute-start(bf16[512,1280]{1,0:T(8,128)(2,1)S(1)} %get-tuple-element.8), channel_id=1, source_target_pairs={{12,8},{13,9},{14,10},{15,11},{28,24},{29,25},{30,26},{31,27}} | collective-permute-start | bytes 3932168 | tf_op jit(solution)/shard_map/ppermute | solution.py:151
  259.9 52.1 %collective-permute-start.5 = (bf16[512,1280]{1,0:T(8,128)(2,1)}, bf16[512,1280]{1,0:T(8,128)(2,1)}, u32[]{:S(2)}, u32[]{:S(2)}) collective-permute-start(bf16[512,1280]{1,0:T(8,128)(2,1)} %fusion.27), channel_id=1, source_target_pairs={{0,4},{4,8},{1,5},{5,9},{2,6},{6,10},{3,7},{7,11},{16,20},{20,24},... | collective-permute-start | bytes 3932168 | tf_op jit(solution)/shard_map/ppermute | solution.py:148
  289.8 33.2 %collective-permute-start.14 = (bf16[512,1280]{1,0:T(8,128)(2,1)}, bf16[512,1280]{1,0:T(8,128)(2,1)S(1)}, u32[]{:S(2)}, u32[]{:S(2)}) collective-permute-start(bf16[512,1280]{1,0:T(8,128)(2,1)} %get-tuple-element.10), channel_id=1, source_target_pairs={{12,8},{8,4},{13,9},{9,5},{14,10},{10,6},{15,11},{11,7},{28,24},{2... | collective-permute-start | bytes 3932168 | tf_op jit(solution)/shard_map/ppermute | solution.py:151
  291.3 26.3 %copy-start.21 = (s32[4]{0:T(128)S(1)}, s32[4]{0:T(128)}, u32[]{:S(2)}) copy-start(s32[4]{0:T(128)} %param.17) | copy-start | bytes 52
  291.3 26.4 %copy-start.11 = (bf16[512,1280]{1,0:T(8,128)(2,1)S(1)}, bf16[512,1280]{1,0:T(8,128)(2,1)}, u32[]{:S(2)}) copy-start(bf16[512,1280]{1,0:T(8,128)(2,1)} %get-tuple-element.9) | copy-start | bytes 3932164
  315.7 35.3 %collective-permute-start.8 = (bf16[512,1280]{1,0:T(8,128)(2,1)S(1)}, bf16[512,1280]{1,0:T(8,128)(2,1)S(1)}, u32[]{:S(2)}, u32[]{:S(2)}) collective-permute-start(bf16[512,1280]{1,0:T(8,128)(2,1)S(1)} %get-tuple-element.6), channel_id=1, source_target_pairs={{12,8},{8,4},{13,9},{9,5},{14,10},{10,6},{15,11},{11,7},{28,24},{2... | collective-permute-start | bytes 3932168 | tf_op jit(solution)/shard_map/ppermute | solution.py:151
  317.7 9.2 %copy-start.24 = (s32[4]{0:T(128)S(1)}, s32[4]{0:T(128)}, u32[]{:S(2)}) copy-start(s32[4]{0:T(128)} %param.16) | copy-start | bytes 52
  317.7 38.3 %collective-permute-start.12 = (bf16[512,1280]{1,0:T(8,128)(2,1)S(1)}, bf16[512,1280]{1,0:T(8,128)(2,1)S(1)}, u32[]{:S(2)}, u32[]{:S(2)}) collective-permute-start(bf16[512,1280]{1,0:T(8,128)(2,1)S(1)} %copy-done.11), channel_id=1, source_target_pairs={{0,4},{4,8},{8,12},{1,5},{5,9},{9,13},{2,6},{6,10},{10,14},{3,7},{... | collective-permute-start | bytes 3932168 | tf_op jit(solution)/shard_map/ppermute | solution.py:148
  325.0 54.2 %collective-permute-start.15 = (bf16[512,1280]{1,0:T(8,128)(2,1)S(1)}, bf16[512,1280]{1,0:T(8,128)(2,1)S(1)}, u32[]{:S(2)}, u32[]{:S(2)}) collective-permute-start(bf16[512,1280]{1,0:T(8,128)(2,1)S(1)} %fusion.21), channel_id=1, source_target_pairs={{12,8},{8,4},{4,0},{13,9},{9,5},{5,1},{14,10},{10,6},{6,2},{15,11}... | collective-permute-start | bytes 3932168 | tf_op jit(solution)/shard_map/ppermute | solution.py:151
  327.6 55.3 %collective-permute-start.6 = (bf16[512,1280]{1,0:T(8,128)(2,1)S(1)}, bf16[512,1280]{1,0:T(8,128)(2,1)S(1)}, u32[]{:S(2)}, u32[]{:S(2)}) collective-permute-start(bf16[512,1280]{1,0:T(8,128)(2,1)S(1)} %get-tuple-element.5), channel_id=1, source_target_pairs={{0,4},{4,8},{8,12},{1,5},{5,9},{9,13},{2,6},{6,10},{10,14},{3,7},{... | collective-permute-start | bytes 3932168 | tf_op jit(solution)/shard_map/ppermute | solution.py:148
  353.1 52.5 %collective-permute-start.9 = (bf16[512,1280]{1,0:T(8,128)(2,1)S(1)}, bf16[512,1280]{1,0:T(8,128)(2,1)S(1)}, u32[]{:S(2)}, u32[]{:S(2)}) collective-permute-start(bf16[512,1280]{1,0:T(8,128)(2,1)S(1)} %fusion.26), channel_id=1, source_target_pairs={{12,8},{8,4},{4,0},{13,9},{9,5},{5,1},{14,10},{10,6},{6,2},{15,11}... | collective-permute-start | bytes 3932168 | tf_op jit(solution)/shard_map/ppermute | solution.py:151
  381.3 1.5 copy-start.2
  407.8 2.2 copy-start.4
  407.8 2.2 slice-start.4
  410.8 2.6 slice-start.5
  415.0 2.4 copy-start.3
  415.0 2.4 copy-start.22
  420.5 1.6 copy-start.7
  420.6 2.2 copy-start.8
  422.8 1.9 copy-start.13
  424.6 7.6 %copy-start.20 = (pred[128,128]{0,1:T(8,128)(4,1)S(1)}, pred[128,128]{0,1:T(8,128)(4,1)}, u32[]{:S(2)}) copy-start(pred[128,128]{0,1:T(8,128)(4,1)} %iota_compare_fusion) | copy-start | bytes 49156
  447.7 1.6 copy-start.23
  447.7 12.2 %slice-start = ((s8[16777216]{0:T(1024)(128)(4,1)}), s8[4194304]{0:T(1024)(128)(4,1)S(1)}, s32[]{:S(2)}) async-start(s8[16777216]{0:T(1024)(128)(4,1)} %bitcast.277), calls=%async_computation.1 | async-start | bytes 8388608
  449.2 10.6 %slice-start.1 = ((s8[16777216]{0:T(1024)(128)(4,1)}), s8[4194304]{0:T(1024)(128)(4,1)S(1)}, s32[]{:S(2)}) async-start(s8[16777216]{0:T(1024)(128)(4,1)} %bitcast.277), calls=%async_computation.2 | async-start | bytes 8388608
  449.2 10.6 %slice-start.2 = ((s8[16777216]{0:T(1024)(128)(4,1)}), s8[4194304]{0:T(1024)(128)(4,1)S(1)}, s32[]{:S(2)}) async-start(s8[16777216]{0:T(1024)(128)(4,1)} %bitcast.277), calls=%async_computation.3 | async-start | bytes 8388608
  449.2 10.6 %slice-start.3 = ((s8[16777216]{0:T(1024)(128)(4,1)}), s8[4194304]{0:T(1024)(128)(4,1)S(1)}, s32[]{:S(2)}) async-start(s8[16777216]{0:T(1024)(128)(4,1)} %bitcast.277), calls=%async_computation.4 | async-start | bytes 8388608
  469.3 1.0 copy-start.16
  469.3 1.7 copy-start.14
  469.3 1.7 copy-start.15
  (1 other events, 1.0 us)
Sparse Core Ops, SparseCore 0:
  88.6 81.4 all-gather.3

commit v2 on v0

--- a/solution.py
+++ b/solution.py
@@ -1,6 +1,10 @@
+import functools
+
 import jax
 import jax.numpy as jnp
 from jax import lax
+from jax.experimental import pallas as pl
+from jax.experimental.pallas import tpu as pltpu
 from jax.sharding import PartitionSpec as P
 
 HEAD_DIM = 128
@@ -69,7 +73,7 @@
     return mixed.reshape(session_count * turn_size, head_local * head_dim).astype(jnp.bfloat16)
 
 
-def local(tokens, norm_gain, w_query, w_key, w_value, cache_key, cache_value, turn_len, cache_len):
+def local_gather(tokens, norm_gain, w_query, w_key, w_value, cache_key, cache_value, turn_len, cache_len):
     gathered = lax.all_gather(tokens, "head", axis=1, tiled=True)
     widened = gathered.astype(jnp.float32)
     inverse_rms = lax.rsqrt(jnp.mean(widened * widened, axis=1, keepdims=True) + EPSILON)
@@ -110,6 +114,398 @@
     )
 
 
+def column_of(row):
+    lanes = row.shape[1]
+    return jnp.transpose(jnp.broadcast_to(row, (lanes, lanes)))[:, :1]
+
+
+def row_of(column):
+    lanes = column.shape[0]
+    return jnp.transpose(jnp.broadcast_to(column, (lanes, lanes)))[:8, :]
+
+
+def move_kernel(
+    width,
+    tokens_ref,
+    gain_ref,
+    out_ref,
+    stage,
+    mine,
+    sums,
+    piece_send,
+    piece_recv,
+    self_sem,
+    sums_send,
+    sums_recv,
+    pair_send,
+    pair_recv,
+    cross_send,
+    cross_recv,
+    pass_send,
+    pass_recv,
+    own_sem,
+):
+    ways, rows = stage.shape[0], stage.shape[1]
+    w_at, h_at = lax.axis_index("wloop"), lax.axis_index("head")
+
+    def device(w, h):
+        return {"wloop": w, "head": h}
+
+    barrier = pltpu.get_barrier_semaphore()
+    for dw in range(ways):
+        for dh in range(ways):
+            if dw or dh:
+                pl.semaphore_signal(
+                    barrier,
+                    inc=1,
+                    device_id=device(lax.rem(w_at + dw, ways), lax.rem(h_at + dh, ways)),
+                    device_id_type=pl.DeviceIdType.MESH,
+                )
+    pl.semaphore_wait(barrier, ways * ways - 1)
+
+    def remote(source, target, send, recv, w, h):
+        return pltpu.make_async_remote_copy(
+            src_ref=source,
+            dst_ref=target,
+            send_sem=send,
+            recv_sem=recv,
+            device_id=device(w, h),
+            device_id_type=pl.DeviceIdType.MESH,
+        )
+
+    pieces = []
+    for j in range(ways):
+        to = lax.rem(w_at + j, ways)
+        source = tokens_ref.at[pl.ds(pl.multiple_of(to * rows, rows), rows), :]
+        pieces.append(
+            remote(source, stage.at[w_at], piece_send.at[j], piece_recv.at[j], h_at, to)
+        )
+    kept = pltpu.make_async_copy(
+        tokens_ref.at[pl.ds(pl.multiple_of(w_at * rows, rows), rows), :],
+        stage.at[w_at],
+        self_sem,
+    )
+
+    @pl.when(w_at != h_at)
+    def _():
+        pieces[0].start()
+
+    @pl.when(w_at == h_at)
+    def _():
+        kept.start()
+
+    for j in range(1, ways):
+        pieces[j].start()
+
+    sibling = h_at + 1 - 2 * lax.rem(h_at, 2)
+    partner = lax.rem(h_at + ways // 2, ways)
+
+    def block_of(j):
+        return lax.rem(h_at + ways - j, ways)
+
+    exchanges = [
+        [
+            remote(
+                sums.at[j, w_at],
+                sums.at[j, w_at],
+                sums_send.at[j, k - 1],
+                sums_recv.at[j, k - 1],
+                lax.rem(w_at + k, ways),
+                h_at,
+            )
+            for k in range(1, ways)
+        ]
+        for j in range(ways)
+    ]
+    sends = []
+    for j in range(ways):
+        block = block_of(j)
+        sends.append(
+            (
+                pltpu.make_async_copy(mine.at[block], out_ref.at[block, h_at], own_sem.at[j]),
+                remote(
+                    mine.at[block],
+                    out_ref.at[block, h_at],
+                    cross_send.at[j],
+                    cross_recv.at[j],
+                    w_at,
+                    partner,
+                ),
+                remote(
+                    mine.at[block],
+                    out_ref.at[block, h_at],
+                    pair_send.at[j],
+                    pair_recv.at[j],
+                    w_at,
+                    sibling,
+                ),
+            )
+        )
+
+    def take_in(j):
+        if j == 0:
+
+            @pl.when(w_at != h_at)
+            def _():
+                pieces[0].wait_recv()
+
+            @pl.when(w_at == h_at)
+            def _():
+                kept.wait()
+        else:
+            pieces[j].wait_recv()
+        total = None
+        held = stage[block_of(j)].astype(jnp.float32)
+        total = jnp.sum(held * held, axis=1, keepdims=True)
+        sums[j, w_at] = row_of(total)
+        for exchange in exchanges[j]:
+            exchange.start()
+
+    def give_out(j):
+        for exchange in exchanges[j]:
+            exchange.wait_recv()
+        total = sums[j, 0]
+        for w in range(1, ways):
+            total = total + sums[j, w]
+        inverse = column_of(lax.rsqrt(total[:1] / width + EPSILON))
+        block = block_of(j)
+        held = stage[block].astype(jnp.float32)
+        mine[block] = (held * inverse * gain_ref[...]).astype(jnp.bfloat16)
+        for copy in reversed(sends[j]):
+            copy.start()
+
+    take_in(0)
+    for j in range(1, ways):
+        take_in(j)
+        give_out(j - 1)
+    give_out(ways - 1)
+
+    passes = []
+    for j in range(ways):
+        block = lax.rem(partner + ways - j, ways)
+        sends[j][1].wait_recv()
+        passed = remote(
+            out_ref.at[block, partner],
+            out_ref.at[block, partner],
+            pass_send.at[j],
+            pass_recv.at[j],
+            w_at,
+            sibling,
+        )
+        passed.start()
+        passes.append(passed)
+    for j in range(ways):
+        sends[j][0].wait()
+        sends[j][1].wait_send()
+        sends[j][2].wait()
+        passes[j].wait()
+        for exchange in exchanges[j]:
+            exchange.wait_send()
+        if j:
+            pieces[j].wait_send()
+
+    @pl.when(w_at != h_at)
+    def _():
+        pieces[0].wait_send()
+
+
+def moved_normed(tokens, gain, width, ways):
+    row_count, depth = tokens.shape
+    rows = row_count // ways
+    pair = pltpu.SemaphoreType.DMA((ways,))
+    grid = pltpu.SemaphoreType.DMA((ways, ways - 1))
+    moved = pl.pallas_call(
+        functools.partial(move_kernel, width),
+        out_shape=jax.ShapeDtypeStruct((ways, ways, rows, depth), jnp.bfloat16),
+        in_specs=[
+            pl.BlockSpec(memory_space=pl.ANY),
+            pl.BlockSpec(memory_space=pltpu.VMEM),
+        ],
+        out_specs=pl.BlockSpec(memory_space=pl.ANY),
+        scratch_shapes=[
+            pltpu.VMEM((ways, rows, depth), jnp.bfloat16),
+            pltpu.VMEM((ways, rows, depth), jnp.bfloat16),
+            pltpu.VMEM((ways, ways, 8, rows), jnp.float32),
+            pair,
+            pair,
+            pltpu.SemaphoreType.DMA,
+            grid,
+            grid,
+            pair,
+            pair,
+            pair,
+            pair,
+            pair,
+            pair,
+            pair,
+        ],
+        compiler_params=pltpu.CompilerParams(
+            collective_id=0, has_side_effects=True, vmem_limit_bytes=24 * 1024 * 1024
+        ),
+    )(tokens, gain.reshape(1, depth))
+    return moved.reshape(ways, row_count, depth)
+
+
+def attend_kernel(
+    group_size, turn_len_ref, cache_len_ref, q_ref, kv_ref, cos_ref, sin_ref, old_k_ref, old_v_ref,
+    out_ref, new_k_ref, new_v_ref,
+):
+    at = pl.program_id(0)
+    turn_size, head_dim = cos_ref.shape
+    cache_size = old_k_ref.shape[1]
+    cosine, sine = cos_ref[...], sin_ref[...]
+
+    def turned(v):
+        return v * cosine + pltpu.roll(v, head_dim // 2, 1) * sine
+
+    live = lax.broadcasted_iota(jnp.int32, (turn_size, head_dim), 0) < turn_len_ref[at]
+    new_k = jnp.where(live, turned(kv_ref[:, :head_dim]), 0.0).astype(jnp.bfloat16)
+    new_v = jnp.where(live, kv_ref[:, head_dim:], 0.0).astype(jnp.bfloat16)
+    new_k_ref[...] = new_k
+    new_v_ref[...] = new_v
+    old_k, old_v = old_k_ref[0], old_v_ref[0]
+    slot_live = lax.broadcasted_iota(jnp.int32, (1, cache_size), 1) < cache_len_ref[at]
+    bias = jnp.where(slot_live, 0.0, -jnp.inf)
+    causal = lax.broadcasted_iota(jnp.int32, (turn_size, turn_size), 1) <= (
+        lax.broadcasted_iota(jnp.int32, (turn_size, turn_size), 0)
+    )
+    factor = head_dim ** (-0.5)
+    contract = (((1,), (1,)), ((), ()))
+    for head in range(group_size):
+        cols = slice(head * head_dim, (head + 1) * head_dim)
+        query = turned(q_ref[:, cols]).astype(jnp.bfloat16)
+        far = lax.dot_general(query, old_k, contract, preferred_element_type=jnp.float32)
+        near = lax.dot_general(query, new_k, contract, preferred_element_type=jnp.float32)
+        far = far * factor + bias
+        near = jnp.where(causal, near * factor, -jnp.inf)
+        top = jnp.maximum(
+            jnp.max(far, axis=1, keepdims=True), jnp.max(near, axis=1, keepdims=True)
+        )
+        far = jnp.exp(far - top)
+        near = jnp.exp(near - top)
+        total = jnp.sum(far, axis=1, keepdims=True) + jnp.sum(near, axis=1, keepdims=True)
+        scale = 1.0 / total
+        mixed = jnp.dot(
+            (far * scale).astype(jnp.bfloat16), old_v, preferred_element_type=jnp.float32
+        ) + jnp.dot((near * scale).astype(jnp.bfloat16), new_v, preferred_element_type=jnp.float32)
+        out_ref[:, cols] = jnp.where(live, mixed, 0.0).astype(jnp.bfloat16)
+
+
+def attend_part(summed, cosine, sine, cache_key, cache_value, turn_len, cache_len, kv):
+    row_count, width = summed.shape
+    sessions, cache_size, _ = cache_key.shape
+    turn_size = row_count // sessions
+    q_cols = width - 2 * HEAD_DIM
+    smem = pl.BlockSpec(memory_space=pltpu.SMEM)
+    rows = lambda cols, at=0: pl.BlockSpec((turn_size, cols), lambda s: (s, at))
+    cached = pl.BlockSpec((1, cache_size, HEAD_DIM), lambda s: (s, 0, kv))
+    bf16 = lambda cols: jax.ShapeDtypeStruct((row_count, cols), jnp.bfloat16)
+    work = row_count * q_cols * (cache_size + turn_size)
+    return pl.pallas_call(
+        functools.partial(attend_kernel, q_cols // HEAD_DIM),
+        grid=(sessions,),
+        out_shape=(bf16(q_cols), bf16(HEAD_DIM), bf16(HEAD_DIM)),
+        in_specs=[
+            smem,
+            smem,
+            rows(q_cols),
+            rows(2 * HEAD_DIM, q_cols // (2 * HEAD_DIM)),
+            rows(HEAD_DIM),
+            rows(HEAD_DIM),
+            cached,
+            cached,
+        ],
+        out_specs=(rows(q_cols), rows(HEAD_DIM), rows(HEAD_DIM)),
+        compiler_params=pltpu.CompilerParams(vmem_limit_bytes=32 * 1024 * 1024),
+        cost_estimate=pl.CostEstimate(
+            flops=16 * work, bytes_accessed=10**7, transcendentals=work // HEAD_DIM
+        ),
+    )(turn_len, cache_len, summed, summed, cosine, sine, cache_key, cache_value)
+
+
+def reduce_over_line(partials, ways, after):
+    w_at = lax.axis_index("wloop")
+
+    def pick(index):
+        return lax.dynamic_index_in_dim(
+            partials, jnp.clip(index, 0, ways - 1), 0, keepdims=False
+        )
+
+    rising = None
+    falling = None
+    middle = None
+    for step in range(1, ways):
+        up = pick(w_at + ways - step)
+        down = pick(w_at - ways + step)
+        if rising is not None:
+            up = up + rising.astype(jnp.float32)
+            down = down + falling.astype(jnp.float32)
+        up, down = up.astype(jnp.bfloat16), down.astype(jnp.bfloat16)
+        if step == 1 and after is not None:
+            up, down, _ = lax.optimization_barrier((up, down, after))
+        if step == ways - 1:
+            middle = up[:8], down[:8]
+        rising = lax.ppermute(up, "wloop", [(w, w + 1) for w in range(step)])
+        falling = lax.ppermute(
+            down, "wloop", [(ways - 1 - w, ways - 2 - w) for w in range(step)]
+        )
+    summed = pick(w_at) + rising.astype(jnp.float32) + falling.astype(jnp.float32)
+    return summed, middle
+
+
+def local_reduce(
+    tokens, norm_gain, w_query, w_key, w_value, cache_key, cache_value, turn_len, cache_len
+):
+    ways = lax.axis_size("wloop")
+    row_count = tokens.shape[0]
+    depth = w_query.shape[0]
+    width = norm_gain.shape[0]
+    kv_local = w_key.shape[1] // HEAD_DIM
+    q_cols = w_query.shape[1] // kv_local
+    turn_size = row_count // turn_len.shape[0]
+    w_at = lax.axis_index("wloop")
+
+    gain = lax.dynamic_slice_in_dim(norm_gain, w_at * depth, depth, 0)
+    normed = moved_normed(tokens, gain, width, ways)
+
+    half_dim = HEAD_DIM // 2
+    freq_index = jnp.arange(half_dim, dtype=jnp.float32)
+    frequency = jnp.power(jnp.float32(THETA), freq_index * (-2.0 / HEAD_DIM))
+    turn_index = jnp.arange(turn_size, dtype=jnp.int32)
+    positions = (cache_len[:, None] + turn_index[None, :]).astype(jnp.float32)
+    angles = positions.reshape(row_count, 1) * frequency
+    cosine, sine = jnp.cos(angles), jnp.sin(angles)
+    cosine = jnp.concatenate([cosine, cosine], axis=1)
+    sine = jnp.concatenate([-sine, sine], axis=1)
+
+    outs = []
+    after = None
+    for kv in range(kv_local):
+        weights = jnp.concatenate(
+            [
+                w_query[:, kv * q_cols : (kv + 1) * q_cols],
+                w_key[:, kv * HEAD_DIM : (kv + 1) * HEAD_DIM],
+                w_value[:, kv * HEAD_DIM : (kv + 1) * HEAD_DIM],
+            ],
+            axis=1,
+        )
+        partials = jnp.einsum("brd,dn->brn", normed, weights, preferred_element_type=jnp.float32)
+        summed, after = reduce_over_line(partials, ways, after)
+        outs.append(
+            attend_part(summed, cosine, sine, cache_key, cache_value, turn_len, cache_len, kv)
+        )
+    return tuple(jnp.concatenate(arrays, axis=1) for arrays in zip(*outs))
+
+
+def local(*args):
+    tokens, norm_gain = args[0], args[1]
+    w_ways, h_ways = lax.axis_size("wloop"), lax.axis_size("head")
+    if w_ways == h_ways == 4 and tokens.shape[0] == w_ways * HEAD_DIM:
+        if w_ways * tokens.shape[0] < norm_gain.shape[0]:
+            return local_reduce(*args)
+    return local_gather(*args)
+
+
 def solution(mesh):
     placed = (
         P(("grp", "wloop"), "head"),

time: 882 us -> 402 us (0.46)
  waiting for transfers between devices: 754 us -> 120 us
  Pallas kernels: 0 us -> 177 us
  matrix products: 71.1 us -> 26 us
  starting transfers between devices: 0.15 us -> 25.5 us
  between operations: 14 us -> 0.95 us
    all_gather x4 -> x0, waiting for transfers between devices: 752 us -> none  [the longest x1 553 us: local(): lax.all_gather(w_query, 'wloop', axis=0, tiled=True)]
    pallas_call x0 -> x3, Pallas kernels: none -> 177 us  [the longest x1 142 us: moved_normed(): pl.pallas_call(functools.partial(move_kernel, width), out_shape=jax.Shape...]
    ppermute x0 -> x12, waiting for transfers between devices: none -> 120 us  [the longest x6 73.6 us: reduce_over_line(): rising = lax.ppermute(up, 'wloop', [(w, w + 1) for w in range(step)])]
    dot_general x7 -> x2, matrix products: 71.1 us -> 26 us  [local_reduce(): jnp.einsum('brd,dn->brn', normed, weights, preferred_element_type=jnp.flo...]
    ppermute x0 -> x12, starting transfers between devices: none -> 25.5 us  [the longest x6 15.1 us: reduce_over_line(): rising = lax.ppermute(up, 'wloop', [(w, w + 1) for w in range(step)])]
    convert_element_type x1 -> x7, other arithmetic: 0.07 us -> 23.2 us  [the longest x6 23.2 us: reduce_over_line(): up, down = (up.astype(jnp.bfloat16), down.astype(jnp.bfloat16))]
    reduce_sum x3 -> x0, other arithmetic: 20.8 us -> none  [the longest x1 14.6 us: attend_all(): jnp.sum(far_exp, axis=-1, keepdims=True)]
  transfers between devices with their start and end apart: 4 -> 12, of which waited for: 4 -> 7; matrix products, arithmetic and copies ran while one was open for 3% -> 11% of each run, Pallas kernels for 0% -> 5%
where the time goes in v2:
time: 402 us; the launch traced here: 396 us
  Pallas kernels  177 us (44%)
  waiting for transfers between devices  120 us (30%)
  other arithmetic  31.8 us (8%)
  matrix products  26 us (6%)
  starting transfers between devices  25.5 us (6%)
  local copies, waits for them, and re-layouts  14.8 us (4%)
    pallas_call x1, Pallas kernels, moved_normed(): pl.pallas_call(functools.partial(move_kernel, width), out_shape=jax.Shape...  142 us
    ppermute x6, waiting for transfers between devices, reduce_over_line(): rising = lax.ppermute(up, 'wloop', [(w, w + 1) for w in range(step)])  73.6 us
    ppermute x6, waiting for transfers between devices, reduce_over_line(): lax.ppermute(down, 'wloop', [(ways - 1 - w, ways - 2 - w) for w in range(...  46.2 us
    pallas_call x2, Pallas kernels, attend_part(): pl.pallas_call(functools.partial(attend_kernel, q_cols // HEAD_DIM), grid...  35.6 us
    dot_general x2, matrix products, local_reduce(): jnp.einsum('brd,dn->brn', normed, weights, preferred_element_type=jnp.flo...  26 us
    convert_element_type x6, other arithmetic, reduce_over_line(): up, down = (up.astype(jnp.bfloat16), down.astype(jnp.bfloat16))  23.2 us
    ppermute x6, starting transfers between devices, reduce_over_line(): rising = lax.ppermute(up, 'wloop', [(w, w + 1) for w in range(step)])  15.1 us
    ppermute x6, starting transfers between devices, reduce_over_line(): lax.ppermute(down, 'wloop', [(ways - 1 - w, ways - 2 - w) for w in range(...  10.4 us
  transfers between devices with their start and end apart: 12, of which 7 were waited for; matrix products, arithmetic and copies ran while one was open for 11% of the time, Pallas kernels for 5%

profile of v2, /device:TPU:8, one launch (start us, length us, event | category | flops | bytes accessed | tf_op | source)
XLA Modules:
  0.0 396.1 jit_solution(17037811775231714688)
XLA Ops:
  0.6 6.1 %fusion.27 = (bf16[2048,1024]{1,0:T(8,128)(2,1)}, bf16[2048,1024]{1,0:T(8,128)(2,1)}) fusion(bf16[2048,2048]{1,0:T(8,128)(2,1)} %param.11), kind=kLoop, calls=%fused_computation.52 | loop fusion | bytes 16777216 | tf_op jit(solution)/shard_map/slice | solution.py:486
  6.8 0.7 dynamic_slice.46
  7.5 141.7 %shard_map.112 = bf16[4,4,128,2048]{3,2,1,0:T(8,128)(2,1)S(1)} custom-call(bf16[512,2048]{1,0:T(8,128)(2,1)S(1)} %copy-done, f32[1,2048]{1,0:T(1,128)S(1)} %bitcast.62), custom_call_target="tpu_custom_call" | custom-call | tf_op jit(solution)/shard_map/pallas_call | solution.py:317
  149.2 1.2 fusion.28
  150.3 1.2 copy-done.7
  151.6 11.1 %fusion = f32[4,512,1280]{2,1,0:T(8,128)S(1)} fusion(bf16[4,512,2048]{2,1,0:T(8,128)(2,1)S(1)} %bitcast.60, bf16[2048,128]{1,0:T(8,128)(2,1)S(1)} %get-tuple-element.37, bf16[2048,128]{1,0:T(8,128)(2,1)S(1)} %get-tuple-element.29, bf16[2048,1024]{1,0:T(8,128)(2,1)S(1)} %copy-done.7), kind=kOutput, calls=%fused_computation.1 | convolution fusion | flops 10753146880 | bytes 24117248 | tf_op jit(solution)/shard_map/brd,dn->brn/dot_general | solution.py:492
  162.7 1.4 fusion.20
  164.1 1.5 collective-permute-start
  165.6 2.0 collective-permute-start.3
  167.6 0.4 copy-done.6
  167.9 14.9 %fusion.5 = f32[4,512,1280]{2,1,0:T(8,128)} fusion(bf16[4,512,2048]{2,1,0:T(8,128)(2,1)S(1)} %bitcast.61, bf16[2048,128]{1,0:T(8,128)(2,1)} %get-tuple-element.36, bf16[2048,128]{1,0:T(8,128)(2,1)S(1)} %get-tuple-element.30, bf16[2048,1024]{1,0:T(8,128)(2,1)S(1)} %copy-done.6), kind=kOutput, calls=%fused_computation.7 | convolution fusion | flops 10753146880 | bytes 24117248 | tf_op jit(solution)/shard_map/brd,dn->brn/dot_general | solution.py:492
  182.8 3.8 fusion.23
  186.7 1.3 collective-permute-start.6
  188.0 10.4 %collective-permute-done = bf16[512,1280]{1,0:T(8,128)(2,1)} collective-permute-done((bf16[512,1280]{1,0:T(8,128)(2,1)}, bf16[512,1280]{1,0:T(8,128)(2,1)}, u32[]{:S(2)}, u32[]{:S(2)}) %collective-permute-start) | collective-permute-done | bytes 1310752 | tf_op jit(solution)/shard_map/ppermute | solution.py:448
  198.4 3.5 fusion.17
  201.8 1.9 collective-permute-start.1
  203.7 1.8 collective-permute-start.9
  205.5 20.9 %collective-permute-done.6 = bf16[512,1280]{1,0:T(8,128)(2,1)} collective-permute-done((bf16[512,1280]{1,0:T(8,128)(2,1)}, bf16[512,1280]{1,0:T(8,128)(2,1)}, u32[]{:S(2)}, u32[]{:S(2)}) %collective-permute-start.6) | collective-permute-done | bytes 1310752 | tf_op jit(solution)/shard_map/ppermute | solution.py:448
  226.4 3.5 fusion.12
  229.9 1.9 collective-permute-start.7
  231.8 22.7 %collective-permute-done.1 = bf16[512,1280]{1,0:T(8,128)(2,1)} collective-permute-done((bf16[512,1280]{1,0:T(8,128)(2,1)}, bf16[512,1280]{1,0:T(8,128)(2,1)}, u32[]{:S(2)}, u32[]{:S(2)}) %collective-permute-start.1) | collective-permute-done | bytes 1310752 | tf_op jit(solution)/shard_map/ppermute | solution.py:448
  254.5 5.3 %fusion.18 = (bf16[512,1280]{1,0:T(8,128)(2,1)}, bf16[512,1280]{1,0:T(8,128)(2,1)}) fusion(bf16[512,1280]{1,0:T(8,128)(2,1)} %collective-permute-done.1, f32[4,512,1280]{2,1,0:T(8,128)} %copy-done.5, s32[]{:T(128)S(6)} %min.30, bf16[512,1280]{1,0:T(8,128)(2,1)} %collective-permute-done.3, s32[]{:T(128)S(6)} %min.34), kind=kLoop, calls=%fused_computation.29 | loop fusion | flops 3932160 | bytes 10485768 | tf_op jit(solution)/shard_map/convert_element_type | solution.py:443
  259.9 1.3 collective-permute-start.4
  261.2 19.6 %collective-permute-done.7 = bf16[512,1280]{1,0:T(8,128)(2,1)} collective-permute-done((bf16[512,1280]{1,0:T(8,128)(2,1)}, bf16[512,1280]{1,0:T(8,128)(2,1)}, u32[]{:S(2)}, u32[]{:S(2)}) %collective-permute-start.7) | collective-permute-done | bytes 1310752 | tf_op jit(solution)/shard_map/ppermute | solution.py:448
  280.7 5.3 %fusion.13 = (bf16[512,1280]{1,0:T(8,128)(2,1)}, bf16[512,1280]{1,0:T(8,128)(2,1)}) fusion(bf16[512,1280]{1,0:T(8,128)(2,1)} %collective-permute-done.7, f32[4,512,1280]{2,1,0:T(8,128)} %fusion.5, s32[]{:T(128)S(6)} %min.30, bf16[512,1280]{1,0:T(8,128)(2,1)} %collective-permute-done.9, s32[]{:T(128)S(6)} %min.34), kind=kLoop, calls=%fused_computation.19 | loop fusion | flops 3932160 | bytes 10485768 | tf_op jit(solution)/shard_map/convert_element_type | solution.py:443
  286.1 1.3 collective-permute-start.10
  287.4 0.0 copy-start.1
  287.4 4.6 %collective-permute-start.2 = (bf16[512,1280]{1,0:T(8,128)(2,1)}, bf16[512,1280]{1,0:T(8,128)(2,1)S(1)}, u32[]{:S(2)}, u32[]{:S(2)}) collective-permute-start(bf16[512,1280]{1,0:T(8,128)(2,1)} %get-tuple-element.19), channel_id=1, source_target_pairs={{0,4},{4,8},{8,12},{1,5},{5,9},{9,13},{2,6},{6,10},{10,14},{3,7},{... | collective-permute-start | bytes 3932168 | tf_op jit(solution)/shard_map/ppermute | solution.py:448
  292.0 3.2 fusion.16
  295.2 1.9 collective-permute-start.5
  297.1 0.1 convert_bitcast_fusion
  297.2 1.0 fusion.24
  298.2 0.2 pad_maximum_fusion.1
  298.4 3.9 collective-permute-start.8
  302.3 17.7 %collective-permute-done.10 = bf16[512,1280]{1,0:T(8,128)(2,1)} collective-permute-done((bf16[512,1280]{1,0:T(8,128)(2,1)}, bf16[512,1280]{1,0:T(8,128)(2,1)}, u32[]{:S(2)}, u32[]{:S(2)}) %collective-permute-start.10) | collective-permute-done | bytes 1310752 | tf_op jit(solution)/shard_map/ppermute | solution.py:449
  320.0 2.4 fusion.11
  322.4 0.0 copy-start.2
  322.4 0.0 copy-start.3
  322.4 2.2 collective-permute-start.11
  324.6 23.3 %collective-permute-done.5 = bf16[512,1280]{1,0:T(8,128)(2,1)S(1)} collective-permute-done((bf16[512,1280]{1,0:T(8,128)(2,1)}, bf16[512,1280]{1,0:T(8,128)(2,1)S(1)}, u32[]{:S(2)}, u32[]{:S(2)}) %collective-permute-start.5) | collective-permute-done | bytes 1310752 | tf_op jit(solution)/shard_map/ppermute | solution.py:449
  348.0 2.2 fusion.19.q_ref.kv_ref
  350.2 17.9 %shard_map.113 = (bf16[512,1024]{1,0:T(8,128)(2,1)S(1)}, bf16[512,128]{1,0:T(8,128)(2,1)S(1)}, bf16[512,128]{1,0:T(8,128)(2,1)S(1)}) custom-call(s32[4]{0:T(128)S(1)} %copy-done.4, s32[4]{0:T(128)S(1)} %copy-done.1, f32[512,1280]{1,0:T(8,128)S(1)} %fusion.19.q_ref.kv_ref, f32[512,1280]{1,0:T(8,128)S(1)} %fusion.19.q_ref.kv_ref, ...), custom_call_target="tpu_custom_call" | custom-call | flops 9663676416 | bytes 10000000 | tf_op jit(solution)/shard_map/pallas_call | solution.py:404
  368.1 5.1 %collective-permute-done.11 = bf16[512,1280]{1,0:T(8,128)(2,1)S(1)} collective-permute-done((bf16[512,1280]{1,0:T(8,128)(2,1)S(1)}, bf16[512,1280]{1,0:T(8,128)(2,1)S(1)}, u32[]{:S(2)}, u32[]{:S(2)}) %collective-permute-start.11) | collective-permute-done | bytes 1310752 | tf_op jit(solution)/shard_map/ppermute | solution.py:449
  373.3 2.2 fusion.14.q_ref.kv_ref
  375.4 17.7 %shard_map.114 = (bf16[512,1024]{1,0:T(8,128)(2,1)S(1)}, bf16[512,128]{1,0:T(8,128)(2,1)S(1)}, bf16[512,128]{1,0:T(8,128)(2,1)S(1)}) custom-call(s32[4]{0:T(128)S(1)} %copy-done.4, s32[4]{0:T(128)S(1)} %copy-done.1, f32[512,1280]{1,0:T(8,128)S(1)} %fusion.14.q_ref.kv_ref, f32[512,1280]{1,0:T(8,128)S(1)} %fusion.14.q_ref.kv_ref, ...), custom_call_target="tpu_custom_call" | custom-call | flops 9663676416 | bytes 10000000 | tf_op jit(solution)/shard_map/pallas_call | solution.py:404
  393.2 0.7 pad_maximum_fusion.4
  393.9 0.7 pad_maximum_fusion.3
  394.6 1.5 pad_maximum_fusion
  (21 shorter events, 0.1 us)
Async XLA Ops:
  0.6 6.8 %copy-start = (bf16[512,2048]{1,0:T(8,128)(2,1)S(1)}, bf16[512,2048]{1,0:T(8,128)(2,1)}, u32[]{:S(2)}) copy-start(bf16[512,2048]{1,0:T(8,128)(2,1)} %tokens_ref.1) | copy-start | bytes 6291460
  7.5 141.7 %copy-start.8 = (bf16[2048,256]{1,0:T(8,128)(2,1)S(1)}, bf16[2048,256]{1,0:T(8,128)(2,1)}, u32[]{:S(2)}) copy-start(bf16[2048,256]{1,0:T(8,128)(2,1)} %param.12) | copy-start | bytes 3145732
  7.5 141.7 %copy-start.9 = (bf16[2048,256]{1,0:T(8,128)(2,1)S(1)}, bf16[2048,256]{1,0:T(8,128)(2,1)}, u32[]{:S(2)}) copy-start(bf16[2048,256]{1,0:T(8,128)(2,1)} %param.13) | copy-start | bytes 3145732
  149.2 2.4 copy-start.7
  162.7 20.2 %copy-start.5 = (f32[4,512,1280]{2,1,0:T(8,128)}, f32[4,512,1280]{2,1,0:T(8,128)S(1)}, u32[]{:S(2)}) copy-start(f32[4,512,1280]{2,1,0:T(8,128)S(1)} %fusion) | copy-start | bytes 31457284
  162.7 5.3 %copy-start.6 = (bf16[2048,1024]{1,0:T(8,128)(2,1)S(1)}, bf16[2048,1024]{1,0:T(8,128)(2,1)}, u32[]{:S(2)}) copy-start(bf16[2048,1024]{1,0:T(8,128)(2,1)} %get-tuple-element.28) | copy-start | bytes 12582916
  164.1 34.3 %collective-permute-start = (bf16[512,1280]{1,0:T(8,128)(2,1)}, bf16[512,1280]{1,0:T(8,128)(2,1)}, u32[]{:S(2)}, u32[]{:S(2)}) collective-permute-start(bf16[512,1280]{1,0:T(8,128)(2,1)} %get-tuple-element.21), channel_id=1, source_target_pairs={{0,4},{1,5},{2,6},{3,7},{16,20},{17,21},{18,22},{19,23}} | collective-permute-start | bytes 3932168 | tf_op jit(solution)/shard_map/ppermute | solution.py:448
  165.6 66.2 %collective-permute-start.3 = (bf16[512,1280]{1,0:T(8,128)(2,1)S(1)}, bf16[512,1280]{1,0:T(8,128)(2,1)}, u32[]{:S(2)}, u32[]{:S(2)}) collective-permute-start(bf16[512,1280]{1,0:T(8,128)(2,1)S(1)} %get-tuple-element.22), channel_id=1, source_target_pairs={{12,8},{13,9},{14,10},{15,11},{28,24},{29,25},{30,26},{31,27}} | collective-permute-start | bytes 3932168 | tf_op jit(solution)/shard_map/ppermute | solution.py:449
  186.7 39.8 %collective-permute-start.6 = (bf16[512,1280]{1,0:T(8,128)(2,1)}, bf16[512,1280]{1,0:T(8,128)(2,1)}, u32[]{:S(2)}, u32[]{:S(2)}) collective-permute-start(bf16[512,1280]{1,0:T(8,128)(2,1)} %get-tuple-element.12), channel_id=1, source_target_pairs={{0,4},{1,5},{2,6},{3,7},{16,20},{17,21},{18,22},{19,23}} | collective-permute-start | bytes 3932168 | tf_op jit(solution)/shard_map/ppermute | solution.py:448
  201.8 52.7 %collective-permute-start.1 = (bf16[512,1280]{1,0:T(8,128)(2,1)}, bf16[512,1280]{1,0:T(8,128)(2,1)}, u32[]{:S(2)}, u32[]{:S(2)}) collective-permute-start(bf16[512,1280]{1,0:T(8,128)(2,1)} %fusion.17), channel_id=1, source_target_pairs={{0,4},{4,8},{1,5},{5,9},{2,6},{6,10},{3,7},{7,11},{16,20},{20,24},... | collective-permute-start | bytes 3932168 | tf_op jit(solution)/shard_map/ppermute | solution.py:448
  203.7 57.4 %collective-permute-start.9 = (bf16[512,1280]{1,0:T(8,128)(2,1)S(1)}, bf16[512,1280]{1,0:T(8,128)(2,1)}, u32[]{:S(2)}, u32[]{:S(2)}) collective-permute-start(bf16[512,1280]{1,0:T(8,128)(2,1)S(1)} %get-tuple-element.13), channel_id=1, source_target_pairs={{12,8},{13,9},{14,10},{15,11},{28,24},{29,25},{30,26},{31,27}} | collective-permute-start | bytes 3932168 | tf_op jit(solution)/shard_map/ppermute | solution.py:449
  229.9 50.8 %collective-permute-start.7 = (bf16[512,1280]{1,0:T(8,128)(2,1)}, bf16[512,1280]{1,0:T(8,128)(2,1)}, u32[]{:S(2)}, u32[]{:S(2)}) collective-permute-start(bf16[512,1280]{1,0:T(8,128)(2,1)} %fusion.12), channel_id=1, source_target_pairs={{0,4},{4,8},{1,5},{5,9},{2,6},{6,10},{3,7},{7,11},{16,20},{20,24},... | collective-permute-start | bytes 3932168 | tf_op jit(solution)/shard_map/ppermute | solution.py:448
  259.9 32.1 %collective-permute-start.4 = (bf16[512,1280]{1,0:T(8,128)(2,1)}, bf16[512,1280]{1,0:T(8,128)(2,1)S(1)}, u32[]{:S(2)}, u32[]{:S(2)}) collective-permute-start(bf16[512,1280]{1,0:T(8,128)(2,1)} %get-tuple-element.20), channel_id=1, source_target_pairs={{12,8},{8,4},{13,9},{9,5},{14,10},{10,6},{15,11},{11,7},{28,24},{2... | collective-permute-start | bytes 3932168 | tf_op jit(solution)/shard_map/ppermute | solution.py:449
  286.1 33.9 %collective-permute-start.10 = (bf16[512,1280]{1,0:T(8,128)(2,1)}, bf16[512,1280]{1,0:T(8,128)(2,1)}, u32[]{:S(2)}, u32[]{:S(2)}) collective-permute-start(bf16[512,1280]{1,0:T(8,128)(2,1)} %get-tuple-element.24), channel_id=1, source_target_pairs={{12,8},{8,4},{13,9},{9,5},{14,10},{10,6},{15,11},{11,7},{28,24},{2... | collective-permute-start | bytes 3932168 | tf_op jit(solution)/shard_map/ppermute | solution.py:449
  287.4 9.7 %copy-start.1 = (s32[4]{0:T(128)S(1)}, s32[4]{0:T(128)}, u32[]{:S(2)}) copy-start(s32[4]{0:T(128)} %cache_len_ref.3) | copy-start | bytes 52
  287.4 37.2 %collective-permute-start.2 = (bf16[512,1280]{1,0:T(8,128)(2,1)}, bf16[512,1280]{1,0:T(8,128)(2,1)S(1)}, u32[]{:S(2)}, u32[]{:S(2)}) collective-permute-start(bf16[512,1280]{1,0:T(8,128)(2,1)} %get-tuple-element.19), channel_id=1, source_target_pairs={{0,4},{4,8},{8,12},{1,5},{5,9},{9,13},{2,6},{6,10},{10,14},{3,7},{... | collective-permute-start | bytes 3932168 | tf_op jit(solution)/shard_map/ppermute | solution.py:448
  295.2 52.8 %collective-permute-start.5 = (bf16[512,1280]{1,0:T(8,128)(2,1)}, bf16[512,1280]{1,0:T(8,128)(2,1)S(1)}, u32[]{:S(2)}, u32[]{:S(2)}) collective-permute-start(bf16[512,1280]{1,0:T(8,128)(2,1)} %fusion.16), channel_id=1, source_target_pairs={{12,8},{8,4},{4,0},{13,9},{9,5},{5,1},{14,10},{10,6},{6,2},{15,11}... | collective-permute-start | bytes 3932168 | tf_op jit(solution)/shard_map/ppermute | solution.py:449
  298.4 69.7 %collective-permute-start.8 = (bf16[512,1280]{1,0:T(8,128)(2,1)}, bf16[512,1280]{1,0:T(8,128)(2,1)S(1)}, u32[]{:S(2)}, u32[]{:S(2)}) collective-permute-start(bf16[512,1280]{1,0:T(8,128)(2,1)} %get-tuple-element.23), channel_id=1, source_target_pairs={{0,4},{4,8},{8,12},{1,5},{5,9},{9,13},{2,6},{6,10},{10,14},{3,7},{... | collective-permute-start | bytes 3932168 | tf_op jit(solution)/shard_map/ppermute | solution.py:448
  322.4 27.8 %copy-start.2 = (bf16[4,1024,256]{2,1,0:T(8,128)(2,1)S(1)}, bf16[4,1024,256]{2,1,0:T(8,128)(2,1)}, u32[]{:S(2)}) copy-start(bf16[4,1024,256]{2,1,0:T(8,128)(2,1)} %old_k_ref.3) | copy-start | bytes 6291460
  322.4 27.8 %copy-start.3 = (bf16[4,1024,256]{2,1,0:T(8,128)(2,1)S(1)}, bf16[4,1024,256]{2,1,0:T(8,128)(2,1)}, u32[]{:S(2)}) copy-start(bf16[4,1024,256]{2,1,0:T(8,128)(2,1)} %old_v_ref.3) | copy-start | bytes 6291460
  322.4 27.8 %copy-start.4 = (s32[4]{0:T(128)S(1)}, s32[4]{0:T(128)}, u32[]{:S(2)}) copy-start(s32[4]{0:T(128)} %turn_len_ref.3) | copy-start | bytes 52
  322.4 50.8 %collective-permute-start.11 = (bf16[512,1280]{1,0:T(8,128)(2,1)S(1)}, bf16[512,1280]{1,0:T(8,128)(2,1)S(1)}, u32[]{:S(2)}, u32[]{:S(2)}) collective-permute-start(bf16[512,1280]{1,0:T(8,128)(2,1)S(1)} %fusion.11), channel_id=1, source_target_pairs={{12,8},{8,4},{4,0},{13,9},{9,5},{5,1},{14,10},{10,6},{6,2},{15,11}... | collective-permute-start | bytes 3932168 | tf_op jit(solution)/shard_map/ppermute | solution.py:449

commit v3 on v2

--- a/solution.py
+++ b/solution.py
@@ -130,10 +130,13 @@
     gain_ref,
     out_ref,
     stage,
+    relay,
     mine,
     sums,
     piece_send,
     piece_recv,
+    relay_send,
+    relay_recv,
     self_sem,
     sums_send,
     sums_recv,
@@ -173,32 +176,59 @@
             device_id_type=pl.DeviceIdType.MESH,
         )
 
-    pieces = []
-    for j in range(ways):
-        to = lax.rem(w_at + j, ways)
-        source = tokens_ref.at[pl.ds(pl.multiple_of(to * rows, rows), rows), :]
-        pieces.append(
-            remote(source, stage.at[w_at], piece_send.at[j], piece_recv.at[j], h_at, to)
-        )
-    kept = pltpu.make_async_copy(
-        tokens_ref.at[pl.ds(pl.multiple_of(w_at * rows, rows), rows), :],
-        stage.at[w_at],
-        self_sem,
-    )
+    sibling = h_at + 1 - 2 * lax.rem(h_at, 2)
+    partner = lax.rem(h_at + ways // 2, ways)
+    across = lax.rem(sibling + ways // 2, ways)
+
+    def rows_for(h):
+        return tokens_ref.at[pl.ds(pl.multiple_of(h * rows, rows), rows), :]
+
+    def to_stage(source, at, w, h):
+        return remote(source, stage.at[w_at], piece_send.at[at], piece_recv.at[w_at], w, h)
+
+    crossing = [
+        remote(rows_for(h), relay.at[at], relay_send.at[at], relay_recv.at[at], w_at, partner)
+        for at, h in enumerate((across, partner))
+    ]
+    for copy in crossing:
+        copy.start()
+    beside = to_stage(rows_for(sibling), 0, h_at, sibling)
+    beside.start()
+    straight = to_stage(rows_for(h_at), 1, h_at, h_at)
+    kept = pltpu.make_async_copy(rows_for(h_at), stage.at[w_at], self_sem.at[0])
+    relayed_beside = to_stage(relay.at[0], 2, partner, sibling)
+    relayed = to_stage(relay.at[1], 3, partner, h_at)
+    relay_kept = pltpu.make_async_copy(relay.at[1], stage.at[w_at], self_sem.at[1])
 
     @pl.when(w_at != h_at)
     def _():
-        pieces[0].start()
+        straight.start()
 
     @pl.when(w_at == h_at)
     def _():
         kept.start()
 
-    for j in range(1, ways):
-        pieces[j].start()
-
-    sibling = h_at + 1 - 2 * lax.rem(h_at, 2)
-    partner = lax.rem(h_at + ways // 2, ways)
+    crossing[0].wait_recv()
+    relayed_beside.start()
+    crossing[1].wait_recv()
+
+    @pl.when(w_at != partner)
+    def _():
+        relayed.start()
+
+    @pl.when(w_at == partner)
+    def _():
+        relay_kept.start()
+
+    def arrival(block):
+        return pltpu.make_async_remote_copy(
+            src_ref=stage.at[block],
+            dst_ref=stage.at[block],
+            send_sem=piece_send.at[0],
+            recv_sem=piece_recv.at[block],
+            device_id=device(w_at, sibling),
+            device_id_type=pl.DeviceIdType.MESH,
+        )
 
     def block_of(j):
         return lax.rem(h_at + ways - j, ways)
@@ -243,19 +273,22 @@
         )
 
     def take_in(j):
-        if j == 0:
-
-            @pl.when(w_at != h_at)
-            def _():
-                pieces[0].wait_recv()
-
-            @pl.when(w_at == h_at)
-            def _():
-                kept.wait()
-        else:
-            pieces[j].wait_recv()
-        total = None
-        held = stage[block_of(j)].astype(jnp.float32)
+        block = block_of(j)
+        own = jnp.logical_and(block == w_at, lax.rem(h_at, ways // 2) == lax.rem(w_at, ways // 2))
+
+        @pl.when(jnp.logical_not(own))
+        def _():
+            arrival(block).wait_recv()
+
+        @pl.when(jnp.logical_and(own, w_at == h_at))
+        def _():
+            kept.wait()
+
+        @pl.when(jnp.logical_and(own, w_at != h_at))
+        def _():
+            relay_kept.wait()
+
+        held = stage[block].astype(jnp.float32)
         total = jnp.sum(held * held, axis=1, keepdims=True)
         sums[j, w_at] = row_of(total)
         for exchange in exchanges[j]:
@@ -301,12 +334,18 @@
         passes[j].wait()
         for exchange in exchanges[j]:
             exchange.wait_send()
-        if j:
-            pieces[j].wait_send()
+    beside.wait_send()
+    relayed_beside.wait_send()
+    for copy in crossing:
+        copy.wait_send()
 
     @pl.when(w_at != h_at)
     def _():
-        pieces[0].wait_send()
+        straight.wait_send()
+
+    @pl.when(w_at != partner)
+    def _():
+        relayed.wait_send()
 
 
 def moved_normed(tokens, gain, width, ways):
@@ -324,11 +363,14 @@
         out_specs=pl.BlockSpec(memory_space=pl.ANY),
         scratch_shapes=[
             pltpu.VMEM((ways, rows, depth), jnp.bfloat16),
+            pltpu.VMEM((2, rows, depth), jnp.bfloat16),
             pltpu.VMEM((ways, rows, depth), jnp.bfloat16),
             pltpu.VMEM((ways, ways, 8, rows), jnp.float32),
             pair,
             pair,
-            pltpu.SemaphoreType.DMA,
+            pltpu.SemaphoreType.DMA((2,)),
+            pltpu.SemaphoreType.DMA((2,)),
+            pltpu.SemaphoreType.DMA((2,)),
             grid,
             grid,
             pair,
@@ -366,29 +408,33 @@
     old_k, old_v = old_k_ref[0], old_v_ref[0]
     slot_live = lax.broadcasted_iota(jnp.int32, (1, cache_size), 1) < cache_len_ref[at]
     bias = jnp.where(slot_live, 0.0, -jnp.inf)
+    stack = 2 if group_size % 2 == 0 else 1
     causal = lax.broadcasted_iota(jnp.int32, (turn_size, turn_size), 1) <= (
         lax.broadcasted_iota(jnp.int32, (turn_size, turn_size), 0)
     )
+    near_bias = jnp.concatenate([jnp.where(causal, 0.0, -jnp.inf)] * stack, axis=0)
     factor = head_dim ** (-0.5)
     contract = (((1,), (1,)), ((), ()))
-    for head in range(group_size):
-        cols = slice(head * head_dim, (head + 1) * head_dim)
-        query = turned(q_ref[:, cols]).astype(jnp.bfloat16)
+    for first in range(0, group_size, stack):
+        cols = [slice(h * head_dim, (h + 1) * head_dim) for h in range(first, first + stack)]
+        query = jnp.concatenate([turned(q_ref[:, c]) for c in cols], axis=0).astype(jnp.bfloat16)
         far = lax.dot_general(query, old_k, contract, preferred_element_type=jnp.float32)
         near = lax.dot_general(query, new_k, contract, preferred_element_type=jnp.float32)
         far = far * factor + bias
-        near = jnp.where(causal, near * factor, -jnp.inf)
+        near = near * factor + near_bias
         top = jnp.maximum(
             jnp.max(far, axis=1, keepdims=True), jnp.max(near, axis=1, keepdims=True)
         )
         far = jnp.exp(far - top)
         near = jnp.exp(near - top)
         total = jnp.sum(far, axis=1, keepdims=True) + jnp.sum(near, axis=1, keepdims=True)
-        scale = 1.0 / total
         mixed = jnp.dot(
-            (far * scale).astype(jnp.bfloat16), old_v, preferred_element_type=jnp.float32
-        ) + jnp.dot((near * scale).astype(jnp.bfloat16), new_v, preferred_element_type=jnp.float32)
-        out_ref[:, cols] = jnp.where(live, mixed, 0.0).astype(jnp.bfloat16)
+            far.astype(jnp.bfloat16), old_v, preferred_element_type=jnp.float32
+        ) + jnp.dot(near.astype(jnp.bfloat16), new_v, preferred_element_type=jnp.float32)
+        mixed = mixed * (1.0 / total)
+        for at, c in enumerate(cols):
+            block = mixed[at * turn_size : (at + 1) * turn_size]
+            out_ref[:, c] = jnp.where(live, block, 0.0).astype(jnp.bfloat16)
 
 
 def attend_part(summed, cosine, sine, cache_key, cache_value, turn_len, cache_len, kv):
@@ -423,6 +469,11 @@
     )(turn_len, cache_len, summed, summed, cosine, sine, cache_key, cache_value)
 
 
+def zero_after(array):
+    first = array[(0,) * array.ndim]
+    return (first > jnp.inf).astype(jnp.int32)
+
+
 def reduce_over_line(partials, ways, after):
     w_at = lax.axis_index("wloop")
 
@@ -435,16 +486,15 @@
     falling = None
     middle = None
     for step in range(1, ways):
-        up = pick(w_at + ways - step)
-        down = pick(w_at - ways + step)
+        hold = zero_after(after) if step == 1 and after is not None else 0
+        up = pick(w_at + ways - step + hold)
+        down = pick(w_at - ways + step + hold)
         if rising is not None:
             up = up + rising.astype(jnp.float32)
             down = down + falling.astype(jnp.float32)
+            if middle is None:
+                middle = rising
         up, down = up.astype(jnp.bfloat16), down.astype(jnp.bfloat16)
-        if step == 1 and after is not None:
-            up, down, _ = lax.optimization_barrier((up, down, after))
-        if step == ways - 1:
-            middle = up[:8], down[:8]
         rising = lax.ppermute(up, "wloop", [(w, w + 1) for w in range(step)])
         falling = lax.ppermute(
             down, "wloop", [(ways - 1 - w, ways - 2 - w) for w in range(step)]
@@ -472,7 +522,8 @@
     freq_index = jnp.arange(half_dim, dtype=jnp.float32)
     frequency = jnp.power(jnp.float32(THETA), freq_index * (-2.0 / HEAD_DIM))
     turn_index = jnp.arange(turn_size, dtype=jnp.int32)
-    positions = (cache_len[:, None] + turn_index[None, :]).astype(jnp.float32)
+    starts = cache_len + zero_after(normed)
+    positions = (starts[:, None] + turn_index[None, :]).astype(jnp.float32)
     angles = positions.reshape(row_count, 1) * frequency
     cosine, sine = jnp.cos(angles), jnp.sin(angles)
     cosine = jnp.concatenate([cosine, cosine], axis=1)

time: 402 us -> 378 us (0.940); the launches traced: 396 us -> 378 us
  Pallas kernels: 177 us -> 134 us
  waiting for transfers between devices: 120 us -> 135 us
  local copies, waits for them, and re-layouts: 14.8 us -> 22.7 us
    pallas_call x1, Pallas kernels: 142 us -> 113 us  [moved_normed(): pl.pallas_call(functools.partial(move_kernel, width), out_shape=jax.Shape...]
    pallas_call x2, Pallas kernels: 35.6 us -> 21.8 us  [attend_part(): pl.pallas_call(functools.partial(attend_kernel, q_cols // HEAD_DIM), grid...]
    ppermute x6, waiting for transfers between devices: 46.2 us -> 56.1 us  [reduce_over_line(): lax.ppermute(down, 'wloop', [(ways - 1 - w, ways - 2 - w) for w in range(...]
    unnamed x20 -> x22, local copies, waits for them, and re-layouts: 1.62 us -> 8.01 us
    ppermute x6, waiting for transfers between devices: 73.6 us -> 78.7 us  [reduce_over_line(): rising = lax.ppermute(up, 'wloop', [(w, w + 1) for w in range(step)])]
  transfers between devices with their start and end apart: 12 -> 12, of which waited for: 7 -> 8; matrix products, arithmetic and copies ran while one was open for 11% -> 13% of each run, Pallas kernels for 5% -> 3%
where the time goes in v3:
time: 378 us
  waiting for transfers between devices  135 us (36%)
  Pallas kernels  134 us (35%)
  other arithmetic  32 us (8%)
  matrix products  25.8 us (7%)
  starting transfers between devices  25.6 us (7%)
  local copies, waits for them, and re-layouts  22.7 us (6%)
    pallas_call x1, Pallas kernels, moved_normed(): pl.pallas_call(functools.partial(move_kernel, width), out_shape=jax.Shape...  113 us
    ppermute x6, waiting for transfers between devices, reduce_over_line(): rising = lax.ppermute(up, 'wloop', [(w, w + 1) for w in range(step)])  78.7 us
    ppermute x6, waiting for transfers between devices, reduce_over_line(): lax.ppermute(down, 'wloop', [(ways - 1 - w, ways - 2 - w) for w in range(...  56.1 us
    dot_general x2, matrix products, local_reduce(): jnp.einsum('brd,dn->brn', normed, weights, preferred_element_type=jnp.flo...  25.8 us
    convert_element_type x6, other arithmetic, reduce_over_line(): up, down = (up.astype(jnp.bfloat16), down.astype(jnp.bfloat16))  23.4 us
    pallas_call x2, Pallas kernels, attend_part(): pl.pallas_call(functools.partial(attend_kernel, q_cols // HEAD_DIM), grid...  21.8 us
    ppermute x6, starting transfers between devices, reduce_over_line(): rising = lax.ppermute(up, 'wloop', [(w, w + 1) for w in range(step)])  15.3 us
    ppermute x6, starting transfers between devices, reduce_over_line(): lax.ppermute(down, 'wloop', [(ways - 1 - w, ways - 2 - w) for w in range(...  10.3 us
  transfers between devices with their start and end apart: 12, of which 8 were waited for; matrix products, arithmetic and copies ran while one was open for 13% of the time, Pallas kernels for 3%

profile of v3, /device:TPU:8, one launch (start us, length us, event | category | flops | bytes accessed | tf_op | source)
XLA Modules:
  0.0 377.6 jit_solution(17129396147852838290)
XLA Ops:
  0.6 6.2 %fusion.27 = (bf16[2048,1024]{1,0:T(8,128)(2,1)}, bf16[2048,1024]{1,0:T(8,128)(2,1)}) fusion(bf16[2048,2048]{1,0:T(8,128)(2,1)} %param.11), kind=kLoop, calls=%fused_computation.53 | loop fusion | bytes 16777216 | tf_op jit(solution)/shard_map/slice | solution.py:537
  6.9 0.7 dynamic_slice.46
  7.6 112.7 %shard_map.112 = bf16[4,4,128,2048]{3,2,1,0:T(8,128)(2,1)S(1)} custom-call(bf16[512,2048]{1,0:T(8,128)(2,1)S(1)} %copy-done.1, f32[1,2048]{1,0:T(1,128)S(1)} %bitcast.65), custom_call_target="tpu_custom_call" | custom-call | tf_op jit(solution)/shard_map/pallas_call | solution.py:356
  120.3 1.3 fusion.28
  121.6 4.0 %copy-done.8 = bf16[2048,1024]{1,0:T(8,128)(2,1)S(1)} copy-done((bf16[2048,1024]{1,0:T(8,128)(2,1)S(1)}, bf16[2048,1024]{1,0:T(8,128)(2,1)}, u32[]{:S(2)}) %copy-start.8) | copy-done | bytes 4194328
  125.6 11.1 %fusion = f32[4,512,1280]{2,1,0:T(8,128)S(1)} fusion(bf16[4,512,2048]{2,1,0:T(8,128)(2,1)S(1)} %bitcast.62, bf16[2048,128]{1,0:T(8,128)(2,1)S(1)} %get-tuple-element.33, bf16[2048,128]{1,0:T(8,128)(2,1)S(1)} %get-tuple-element.25, bf16[2048,1024]{1,0:T(8,128)(2,1)S(1)} %copy-done.8), kind=kOutput, calls=%fused_computation.1 | convolution fusion | flops 10753146880 | bytes 24117248 | tf_op jit(solution)/shard_map/brd,dn->brn/dot_general | solution.py:543
  136.7 4.0 %copy-done.6 = f32[4,512,1280]{2,1,0:T(8,128)} copy-done((f32[4,512,1280]{2,1,0:T(8,128)}, f32[4,512,1280]{2,1,0:T(8,128)S(1)}, u32[]{:S(2)}) %copy-start.6) | copy-done | bytes 10485784
  140.7 0.3 fusion.21
  140.9 1.6 collective-permute-start
  142.5 1.7 collective-permute-start.3
  144.3 14.7 %fusion.5 = f32[4,512,1280]{2,1,0:T(8,128)} fusion(bf16[4,512,2048]{2,1,0:T(8,128)(2,1)S(1)} %bitcast.63, bf16[2048,128]{1,0:T(8,128)(2,1)} %get-tuple-element.32, bf16[2048,128]{1,0:T(8,128)(2,1)} %get-tuple-element.26, bf16[2048,1024]{1,0:T(8,128)(2,1)S(1)} %copy-done.7), kind=kOutput, calls=%fused_computation.7 | convolution fusion | flops 10753146880 | bytes 24117248 | tf_op jit(solution)/shard_map/brd,dn->brn/dot_general | solution.py:543
  158.9 15.3 %collective-permute-done = bf16[512,1280]{1,0:T(8,128)(2,1)} collective-permute-done((bf16[512,1280]{1,0:T(8,128)(2,1)S(1)}, bf16[512,1280]{1,0:T(8,128)(2,1)}, u32[]{:S(2)}, u32[]{:S(2)}) %collective-permute-start) | collective-permute-done | bytes 1310752 | tf_op jit(solution)/shard_map/ppermute | solution.py:498
  174.3 1.2 slice.33
  176.1 3.8 %fusion.22 = (bf16[512,1280]{1,0:T(8,128)(2,1)}, bf16[512,1280]{1,0:T(8,128)(2,1)S(1)}) fusion(f32[4,512,1280]{2,1,0:T(8,128)} %fusion.5, s32[]{:T(128)S(6)} %min.40, s32[]{:T(128)S(6)} %min.41), kind=kLoop, calls=%fused_computation.39 | loop fusion | bytes 5242888 | tf_op jit(solution)/shard_map/convert_element_type | solution.py:497
  180.0 1.3 collective-permute-start.6
  181.3 3.4 fusion.17
  184.7 1.9 collective-permute-start.1
  186.6 1.7 collective-permute-start.9
  188.4 25.5 %collective-permute-done.6 = bf16[512,1280]{1,0:T(8,128)(2,1)} collective-permute-done((bf16[512,1280]{1,0:T(8,128)(2,1)}, bf16[512,1280]{1,0:T(8,128)(2,1)}, u32[]{:S(2)}, u32[]{:S(2)}) %collective-permute-start.6) | collective-permute-done | bytes 1310752 | tf_op jit(solution)/shard_map/ppermute | solution.py:498
  213.9 3.5 fusion.12
  217.3 1.9 collective-permute-start.7
  219.2 22.7 %collective-permute-done.1 = bf16[512,1280]{1,0:T(8,128)(2,1)} collective-permute-done((bf16[512,1280]{1,0:T(8,128)(2,1)}, bf16[512,1280]{1,0:T(8,128)(2,1)}, u32[]{:S(2)}, u32[]{:S(2)}) %collective-permute-start.1) | collective-permute-done | bytes 1310752 | tf_op jit(solution)/shard_map/ppermute | solution.py:498
  242.0 5.3 %fusion.18 = (bf16[512,1280]{1,0:T(8,128)(2,1)}, bf16[512,1280]{1,0:T(8,128)(2,1)}) fusion(bf16[512,1280]{1,0:T(8,128)(2,1)} %collective-permute-done.1, f32[4,512,1280]{2,1,0:T(8,128)} %copy-done.6, s32[]{:T(128)S(6)} %min.34, bf16[512,1280]{1,0:T(8,128)(2,1)} %collective-permute-done.3, s32[]{:T(128)S(6)} %min.38), kind=kLoop, calls=%fused_computation.29 | loop fusion | flops 3932160 | bytes 10485768 | tf_op jit(solution)/shard_map/convert_element_type | solution.py:497
  247.2 1.3 collective-permute-start.4
  248.5 1.2 slice.32
  250.3 4.6 %collective-permute-start.2 = (bf16[512,1280]{1,0:T(8,128)(2,1)}, bf16[512,1280]{1,0:T(8,128)(2,1)S(1)}, u32[]{:S(2)}, u32[]{:S(2)}) collective-permute-start(bf16[512,1280]{1,0:T(8,128)(2,1)} %get-tuple-element.15), channel_id=1, source_target_pairs={{0,4},{4,8},{8,12},{1,5},{5,9},{9,13},{2,6},{6,10},{10,14},{3,7},{... | collective-permute-start | bytes 3932168 | tf_op jit(solution)/shard_map/ppermute | solution.py:498
  254.9 15.1 %collective-permute-done.7 = bf16[512,1280]{1,0:T(8,128)(2,1)} collective-permute-done((bf16[512,1280]{1,0:T(8,128)(2,1)}, bf16[512,1280]{1,0:T(8,128)(2,1)}, u32[]{:S(2)}, u32[]{:S(2)}) %collective-permute-start.7) | collective-permute-done | bytes 1310752 | tf_op jit(solution)/shard_map/ppermute | solution.py:498
  270.0 5.3 %fusion.13 = (bf16[512,1280]{1,0:T(8,128)(2,1)}, bf16[512,1280]{1,0:T(8,128)(2,1)}) fusion(bf16[512,1280]{1,0:T(8,128)(2,1)} %collective-permute-done.7, f32[4,512,1280]{2,1,0:T(8,128)} %fusion.5, s32[]{:T(128)S(6)} %min.34, bf16[512,1280]{1,0:T(8,128)(2,1)} %collective-permute-done.9, s32[]{:T(128)S(6)} %min.38), kind=kLoop, calls=%fused_computation.19 | loop fusion | flops 3932160 | bytes 10485768 | tf_op jit(solution)/shard_map/convert_element_type | solution.py:497
  275.4 1.4 collective-permute-start.10
  276.8 0.5 collective-permute-done.4
  277.3 3.5 fusion.16
  280.8 1.9 collective-permute-start.5
  282.7 0.1 convert_bitcast_fusion
  282.8 1.0 fusion.24
  283.8 0.2 pad_maximum_fusion.1
  284.0 4.1 %collective-permute-start.8 = (bf16[512,1280]{1,0:T(8,128)(2,1)}, bf16[512,1280]{1,0:T(8,128)(2,1)S(1)}, u32[]{:S(2)}, u32[]{:S(2)}) collective-permute-start(bf16[512,1280]{1,0:T(8,128)(2,1)} %get-tuple-element.19), channel_id=1, source_target_pairs={{0,4},{4,8},{8,12},{1,5},{5,9},{9,13},{2,6},{6,10},{10,14},{3,7},{... | collective-permute-start | bytes 3932168 | tf_op jit(solution)/shard_map/ppermute | solution.py:498
  288.1 21.3 %collective-permute-done.10 = bf16[512,1280]{1,0:T(8,128)(2,1)} collective-permute-done((bf16[512,1280]{1,0:T(8,128)(2,1)}, bf16[512,1280]{1,0:T(8,128)(2,1)}, u32[]{:S(2)}, u32[]{:S(2)}) %collective-permute-start.10) | collective-permute-done | bytes 1310752 | tf_op jit(solution)/shard_map/ppermute | solution.py:499
  309.4 2.4 fusion.11
  311.9 2.2 collective-permute-start.11
  314.1 23.3 %collective-permute-done.5 = bf16[512,1280]{1,0:T(8,128)(2,1)S(1)} collective-permute-done((bf16[512,1280]{1,0:T(8,128)(2,1)}, bf16[512,1280]{1,0:T(8,128)(2,1)S(1)}, u32[]{:S(2)}, u32[]{:S(2)}) %collective-permute-start.5) | collective-permute-done | bytes 1310752 | tf_op jit(solution)/shard_map/ppermute | solution.py:499
  337.4 2.2 fusion.19.q_ref.kv_ref
  339.6 11.0 %shard_map.113 = (bf16[512,1024]{1,0:T(8,128)(2,1)S(1)}, bf16[512,128]{1,0:T(8,128)(2,1)S(1)}, bf16[512,128]{1,0:T(8,128)(2,1)S(1)}) custom-call(s32[4]{0:T(128)S(1)} %copy-done.4, s32[4]{0:T(128)S(1)} %copy-done.5, f32[512,1280]{1,0:T(8,128)S(1)} %fusion.19.q_ref.kv_ref, f32[512,1280]{1,0:T(8,128)S(1)} %fusion.19.q_ref.kv_ref, ...), custom_call_target="tpu_custom_call" | custom-call | flops 9663676416 | bytes 10000000 | tf_op jit(solution)/shard_map/pallas_call | solution.py:450
  350.6 11.0 %collective-permute-done.11 = bf16[512,1280]{1,0:T(8,128)(2,1)S(1)} collective-permute-done((bf16[512,1280]{1,0:T(8,128)(2,1)S(1)}, bf16[512,1280]{1,0:T(8,128)(2,1)S(1)}, u32[]{:S(2)}, u32[]{:S(2)}) %collective-permute-start.11) | collective-permute-done | bytes 1310752 | tf_op jit(solution)/shard_map/ppermute | solution.py:499
  361.6 2.2 fusion.14.q_ref.kv_ref
  363.8 10.8 %shard_map.114 = (bf16[512,1024]{1,0:T(8,128)(2,1)S(1)}, bf16[512,128]{1,0:T(8,128)(2,1)S(1)}, bf16[512,128]{1,0:T(8,128)(2,1)S(1)}) custom-call(s32[4]{0:T(128)S(1)} %copy-done.4, s32[4]{0:T(128)S(1)} %copy-done.5, f32[512,1280]{1,0:T(8,128)S(1)} %fusion.14.q_ref.kv_ref, f32[512,1280]{1,0:T(8,128)S(1)} %fusion.14.q_ref.kv_ref, ...), custom_call_target="tpu_custom_call" | custom-call | flops 9663676416 | bytes 10000000 | tf_op jit(solution)/shard_map/pallas_call | solution.py:450
  374.6 0.7 pad_maximum_fusion.4
  375.3 0.7 pad_maximum_fusion.3
  376.1 1.5 pad_maximum_fusion
  (26 shorter events, 0.1 us)
Async XLA Ops:
  0.6 6.9 %copy-start.1 = (bf16[512,2048]{1,0:T(8,128)(2,1)S(1)}, bf16[512,2048]{1,0:T(8,128)(2,1)}, u32[]{:S(2)}) copy-start(bf16[512,2048]{1,0:T(8,128)(2,1)} %tokens_ref.1) | copy-start | bytes 6291460
  7.6 112.7 %copy-start.9 = (bf16[2048,256]{1,0:T(8,128)(2,1)S(1)}, bf16[2048,256]{1,0:T(8,128)(2,1)}, u32[]{:S(2)}) copy-start(bf16[2048,256]{1,0:T(8,128)(2,1)} %param.12) | copy-start | bytes 3145732
  7.6 112.7 %copy-start.10 = (bf16[2048,256]{1,0:T(8,128)(2,1)S(1)}, bf16[2048,256]{1,0:T(8,128)(2,1)}, u32[]{:S(2)}) copy-start(bf16[2048,256]{1,0:T(8,128)(2,1)} %param.13) | copy-start | bytes 3145732
  120.3 24.0 %copy-start = (bf16[4,4,128,2048]{3,2,1,0:T(8,128)(2,1)}, bf16[4,4,128,2048]{3,2,1,0:T(8,128)(2,1)S(1)}, u32[]{:S(2)}) copy-start(bf16[4,4,128,2048]{3,2,1,0:T(8,128)(2,1)S(1)} %shard_map.112) | copy-start | bytes 25165828
  120.3 5.3 %copy-start.8 = (bf16[2048,1024]{1,0:T(8,128)(2,1)S(1)}, bf16[2048,1024]{1,0:T(8,128)(2,1)}, u32[]{:S(2)}) copy-start(bf16[2048,1024]{1,0:T(8,128)(2,1)} %get-tuple-element.23) | copy-start | bytes 12582916
  136.7 4.0 %copy-start.6 = (f32[4,512,1280]{2,1,0:T(8,128)}, f32[4,512,1280]{2,1,0:T(8,128)S(1)}, u32[]{:S(2)}) copy-start(f32[4,512,1280]{2,1,0:T(8,128)S(1)} %fusion) | copy-start | bytes 31457284
  140.7 3.6 copy-start.7
  140.9 33.3 %collective-permute-start = (bf16[512,1280]{1,0:T(8,128)(2,1)S(1)}, bf16[512,1280]{1,0:T(8,128)(2,1)}, u32[]{:S(2)}, u32[]{:S(2)}) collective-permute-start(bf16[512,1280]{1,0:T(8,128)(2,1)S(1)} %get-tuple-element.18), channel_id=1, source_target_pairs={{0,4},{1,5},{2,6},{3,7},{16,20},{17,21},{18,22},{19,23}} | collective-permute-start | bytes 3932168 | tf_op jit(solution)/shard_map/ppermute | solution.py:498
  142.5 76.7 %collective-permute-start.3 = (bf16[512,1280]{1,0:T(8,128)(2,1)S(1)}, bf16[512,1280]{1,0:T(8,128)(2,1)}, u32[]{:S(2)}, u32[]{:S(2)}) collective-permute-start(bf16[512,1280]{1,0:T(8,128)(2,1)S(1)} %get-tuple-element.17), channel_id=1, source_target_pairs={{12,8},{13,9},{14,10},{15,11},{28,24},{29,25},{30,26},{31,27}} | collective-permute-start | bytes 3932168 | tf_op jit(solution)/shard_map/ppermute | solution.py:499
  180.0 33.9 %collective-permute-start.6 = (bf16[512,1280]{1,0:T(8,128)(2,1)}, bf16[512,1280]{1,0:T(8,128)(2,1)}, u32[]{:S(2)}, u32[]{:S(2)}) collective-permute-start(bf16[512,1280]{1,0:T(8,128)(2,1)} %get-tuple-element.21), channel_id=1, source_target_pairs={{0,4},{1,5},{2,6},{3,7},{16,20},{17,21},{18,22},{19,23}} | collective-permute-start | bytes 3932168 | tf_op jit(solution)/shard_map/ppermute | solution.py:498
  184.7 57.2 %collective-permute-start.1 = (bf16[512,1280]{1,0:T(8,128)(2,1)}, bf16[512,1280]{1,0:T(8,128)(2,1)}, u32[]{:S(2)}, u32[]{:S(2)}) collective-permute-start(bf16[512,1280]{1,0:T(8,128)(2,1)} %fusion.17), channel_id=1, source_target_pairs={{0,4},{4,8},{1,5},{5,9},{2,6},{6,10},{3,7},{7,11},{16,20},{20,24},... | collective-permute-start | bytes 3932168 | tf_op jit(solution)/shard_map/ppermute | solution.py:498
  186.6 68.3 %collective-permute-start.9 = (bf16[512,1280]{1,0:T(8,128)(2,1)S(1)}, bf16[512,1280]{1,0:T(8,128)(2,1)}, u32[]{:S(2)}, u32[]{:S(2)}) collective-permute-start(bf16[512,1280]{1,0:T(8,128)(2,1)S(1)} %get-tuple-element.22), channel_id=1, source_target_pairs={{12,8},{13,9},{14,10},{15,11},{28,24},{29,25},{30,26},{31,27}} | collective-permute-start | bytes 3932168 | tf_op jit(solution)/shard_map/ppermute | solution.py:499
  217.3 52.7 %collective-permute-start.7 = (bf16[512,1280]{1,0:T(8,128)(2,1)}, bf16[512,1280]{1,0:T(8,128)(2,1)}, u32[]{:S(2)}, u32[]{:S(2)}) collective-permute-start(bf16[512,1280]{1,0:T(8,128)(2,1)} %fusion.12), channel_id=1, source_target_pairs={{0,4},{4,8},{1,5},{5,9},{2,6},{6,10},{3,7},{7,11},{16,20},{20,24},... | collective-permute-start | bytes 3932168 | tf_op jit(solution)/shard_map/ppermute | solution.py:498
  247.2 30.1 %collective-permute-start.4 = (bf16[512,1280]{1,0:T(8,128)(2,1)}, bf16[512,1280]{1,0:T(8,128)(2,1)}, u32[]{:S(2)}, u32[]{:S(2)}) collective-permute-start(bf16[512,1280]{1,0:T(8,128)(2,1)} %get-tuple-element.16), channel_id=1, source_target_pairs={{12,8},{8,4},{13,9},{9,5},{14,10},{10,6},{15,11},{11,7},{28,24},{2... | collective-permute-start | bytes 3932168 | tf_op jit(solution)/shard_map/ppermute | solution.py:499
  250.3 63.7 %collective-permute-start.2 = (bf16[512,1280]{1,0:T(8,128)(2,1)}, bf16[512,1280]{1,0:T(8,128)(2,1)S(1)}, u32[]{:S(2)}, u32[]{:S(2)}) collective-permute-start(bf16[512,1280]{1,0:T(8,128)(2,1)} %get-tuple-element.15), channel_id=1, source_target_pairs={{0,4},{4,8},{8,12},{1,5},{5,9},{9,13},{2,6},{6,10},{10,14},{3,7},{... | collective-permute-start | bytes 3932168 | tf_op jit(solution)/shard_map/ppermute | solution.py:498
  275.4 7.3 %copy-start.5 = (s32[4]{0:T(128)S(1)}, s32[4]{0:T(128)}, u32[]{:S(2)}) copy-start(s32[4]{0:T(128)} %cache_len_ref.3) | copy-start | bytes 52
  275.4 34.0 %collective-permute-start.10 = (bf16[512,1280]{1,0:T(8,128)(2,1)}, bf16[512,1280]{1,0:T(8,128)(2,1)}, u32[]{:S(2)}, u32[]{:S(2)}) collective-permute-start(bf16[512,1280]{1,0:T(8,128)(2,1)} %get-tuple-element.20), channel_id=1, source_target_pairs={{12,8},{8,4},{13,9},{9,5},{14,10},{10,6},{15,11},{11,7},{28,24},{2... | collective-permute-start | bytes 3932168 | tf_op jit(solution)/shard_map/ppermute | solution.py:499
  280.8 56.6 %collective-permute-start.5 = (bf16[512,1280]{1,0:T(8,128)(2,1)}, bf16[512,1280]{1,0:T(8,128)(2,1)S(1)}, u32[]{:S(2)}, u32[]{:S(2)}) collective-permute-start(bf16[512,1280]{1,0:T(8,128)(2,1)} %fusion.16), channel_id=1, source_target_pairs={{12,8},{8,4},{4,0},{13,9},{9,5},{5,1},{14,10},{10,6},{6,2},{15,11}... | collective-permute-start | bytes 3932168 | tf_op jit(solution)/shard_map/ppermute | solution.py:499
  284.0 66.6 %collective-permute-start.8 = (bf16[512,1280]{1,0:T(8,128)(2,1)}, bf16[512,1280]{1,0:T(8,128)(2,1)S(1)}, u32[]{:S(2)}, u32[]{:S(2)}) collective-permute-start(bf16[512,1280]{1,0:T(8,128)(2,1)} %get-tuple-element.19), channel_id=1, source_target_pairs={{0,4},{4,8},{8,12},{1,5},{5,9},{9,13},{2,6},{6,10},{10,14},{3,7},{... | collective-permute-start | bytes 3932168 | tf_op jit(solution)/shard_map/ppermute | solution.py:498
  311.8 27.8 %copy-start.2 = (bf16[4,1024,256]{2,1,0:T(8,128)(2,1)S(1)}, bf16[4,1024,256]{2,1,0:T(8,128)(2,1)}, u32[]{:S(2)}) copy-start(bf16[4,1024,256]{2,1,0:T(8,128)(2,1)} %old_k_ref.3) | copy-start | bytes 6291460
  311.8 27.8 %copy-start.3 = (bf16[4,1024,256]{2,1,0:T(8,128)(2,1)S(1)}, bf16[4,1024,256]{2,1,0:T(8,128)(2,1)}, u32[]{:S(2)}) copy-start(bf16[4,1024,256]{2,1,0:T(8,128)(2,1)} %old_v_ref.3) | copy-start | bytes 6291460
  311.9 27.8 %copy-start.4 = (s32[4]{0:T(128)S(1)}, s32[4]{0:T(128)}, u32[]{:S(2)}) copy-start(s32[4]{0:T(128)} %turn_len_ref.3) | copy-start | bytes 52
  311.9 49.8 %collective-permute-start.11 = (bf16[512,1280]{1,0:T(8,128)(2,1)S(1)}, bf16[512,1280]{1,0:T(8,128)(2,1)S(1)}, u32[]{:S(2)}, u32[]{:S(2)}) collective-permute-start(bf16[512,1280]{1,0:T(8,128)(2,1)S(1)} %fusion.11), channel_id=1, source_target_pairs={{12,8},{8,4},{4,0},{13,9},{9,5},{5,1},{14,10},{10,6},{6,2},{15,11}... | collective-permute-start | bytes 3932168 | tf_op jit(solution)/shard_map/ppermute | solution.py:499

commit v4 on v3

--- a/solution.py
+++ b/solution.py
@@ -390,8 +390,9 @@
 
 def attend_kernel(
     group_size, turn_len_ref, cache_len_ref, q_ref, kv_ref, cos_ref, sin_ref, old_k_ref, old_v_ref,
-    out_ref, new_k_ref, new_v_ref,
+    *rest,
 ):
+    out_ref, new_k_ref, new_v_ref = rest[-3:]
     at = pl.program_id(0)
     turn_size, head_dim = cos_ref.shape
     cache_size = old_k_ref.shape[1]
@@ -437,7 +438,9 @@
             out_ref[:, c] = jnp.where(live, block, 0.0).astype(jnp.bfloat16)
 
 
-def attend_part(summed, cosine, sine, cache_key, cache_value, turn_len, cache_len, kv):
+def attend_part(
+    summed, cosine, sine, cache_key, cache_value, turn_len, cache_len, kv, kv_local, filled
+):
     row_count, width = summed.shape
     sessions, cache_size, _ = cache_key.shape
     turn_size = row_count // sessions
@@ -445,7 +448,9 @@
     smem = pl.BlockSpec(memory_space=pltpu.SMEM)
     rows = lambda cols, at=0: pl.BlockSpec((turn_size, cols), lambda s: (s, at))
     cached = pl.BlockSpec((1, cache_size, HEAD_DIM), lambda s: (s, 0, kv))
-    bf16 = lambda cols: jax.ShapeDtypeStruct((row_count, cols), jnp.bfloat16)
+    bf16 = lambda cols: jax.ShapeDtypeStruct((row_count, kv_local * cols), jnp.bfloat16)
+    filled = filled or ()
+    anywhere = pl.BlockSpec(memory_space=pl.ANY)
     work = row_count * q_cols * (cache_size + turn_size)
     return pl.pallas_call(
         functools.partial(attend_kernel, q_cols // HEAD_DIM),
@@ -460,47 +465,51 @@
             rows(HEAD_DIM),
             cached,
             cached,
+            *([anywhere] * len(filled)),
         ],
-        out_specs=(rows(q_cols), rows(HEAD_DIM), rows(HEAD_DIM)),
+        out_specs=(rows(q_cols, kv), rows(HEAD_DIM, kv), rows(HEAD_DIM, kv)),
+        input_output_aliases={8 + at: at for at in range(len(filled))},
         compiler_params=pltpu.CompilerParams(vmem_limit_bytes=32 * 1024 * 1024),
         cost_estimate=pl.CostEstimate(
             flops=16 * work, bytes_accessed=10**7, transcendentals=work // HEAD_DIM
         ),
-    )(turn_len, cache_len, summed, summed, cosine, sine, cache_key, cache_value)
-
-
-def zero_after(array):
-    first = array[(0,) * array.ndim]
-    return (first > jnp.inf).astype(jnp.int32)
-
-
-def reduce_over_line(partials, ways, after):
+    )(turn_len, cache_len, summed, summed, cosine, sine, cache_key, cache_value, *filled)
+
+
+def reduce_over_line(normed, weights, ways):
     w_at = lax.axis_index("wloop")
 
+    def times(rows, spec):
+        return [
+            jnp.einsum(spec, rows, w, preferred_element_type=jnp.float32)[..., kept]
+            for w, kept in weights
+        ]
+
+    first_at = jnp.where(w_at == 0, ways - 1, 0)
+    first_rows = lax.dynamic_index_in_dim(normed, first_at, 0, keepdims=False)
+    first = jnp.concatenate(
+        [part.astype(jnp.bfloat16) for part in times(first_rows, "rd,dn->rn")], axis=1
+    )
+    rising = lax.ppermute(first, "wloop", [(0, 1)])
+    falling = lax.ppermute(first, "wloop", [(ways - 1, ways - 2)])
+    partials = times(normed, "brd,dn->brn")
+
     def pick(index):
-        return lax.dynamic_index_in_dim(
-            partials, jnp.clip(index, 0, ways - 1), 0, keepdims=False
-        )
-
-    rising = None
-    falling = None
-    middle = None
-    for step in range(1, ways):
-        hold = zero_after(after) if step == 1 and after is not None else 0
-        up = pick(w_at + ways - step + hold)
-        down = pick(w_at - ways + step + hold)
-        if rising is not None:
-            up = up + rising.astype(jnp.float32)
-            down = down + falling.astype(jnp.float32)
-            if middle is None:
-                middle = rising
-        up, down = up.astype(jnp.bfloat16), down.astype(jnp.bfloat16)
-        rising = lax.ppermute(up, "wloop", [(w, w + 1) for w in range(step)])
+        index = jnp.clip(index, 0, ways - 1)
+        return jnp.concatenate(
+            [lax.dynamic_index_in_dim(part, index, 0, keepdims=False) for part in partials], axis=1
+        )
+
+    for step in range(2, ways):
+        up = pick(w_at + ways - step) + rising.astype(jnp.float32)
+        down = pick(w_at - ways + step) + falling.astype(jnp.float32)
+        rising = lax.ppermute(
+            up.astype(jnp.bfloat16), "wloop", [(w, w + 1) for w in range(step)]
+        )
         falling = lax.ppermute(
-            down, "wloop", [(ways - 1 - w, ways - 2 - w) for w in range(step)]
-        )
-    summed = pick(w_at) + rising.astype(jnp.float32) + falling.astype(jnp.float32)
-    return summed, middle
+            down.astype(jnp.bfloat16), "wloop", [(ways - 1 - w, ways - 2 - w) for w in range(step)]
+        )
+    return pick(w_at) + rising.astype(jnp.float32) + falling.astype(jnp.float32)
 
 
 def local_reduce(
@@ -522,30 +531,25 @@
     freq_index = jnp.arange(half_dim, dtype=jnp.float32)
     frequency = jnp.power(jnp.float32(THETA), freq_index * (-2.0 / HEAD_DIM))
     turn_index = jnp.arange(turn_size, dtype=jnp.int32)
-    starts = cache_len + zero_after(normed)
-    positions = (starts[:, None] + turn_index[None, :]).astype(jnp.float32)
+    positions = (cache_len[:, None] + turn_index[None, :]).astype(jnp.float32)
     angles = positions.reshape(row_count, 1) * frequency
     cosine, sine = jnp.cos(angles), jnp.sin(angles)
     cosine = jnp.concatenate([cosine, cosine], axis=1)
     sine = jnp.concatenate([-sine, sine], axis=1)
 
-    outs = []
-    after = None
+    outs = None
     for kv in range(kv_local):
-        weights = jnp.concatenate(
-            [
-                w_query[:, kv * q_cols : (kv + 1) * q_cols],
-                w_key[:, kv * HEAD_DIM : (kv + 1) * HEAD_DIM],
-                w_value[:, kv * HEAD_DIM : (kv + 1) * HEAD_DIM],
-            ],
-            axis=1,
-        )
-        partials = jnp.einsum("brd,dn->brn", normed, weights, preferred_element_type=jnp.float32)
-        summed, after = reduce_over_line(partials, ways, after)
-        outs.append(
-            attend_part(summed, cosine, sine, cache_key, cache_value, turn_len, cache_len, kv)
-        )
-    return tuple(jnp.concatenate(arrays, axis=1) for arrays in zip(*outs))
+        heads = slice(kv * HEAD_DIM, (kv + 1) * HEAD_DIM)
+        weights = (
+            (w_query[:, kv * q_cols : (kv + 1) * q_cols], slice(None)),
+            (w_key, heads),
+            (w_value, heads),
+        )
+        summed = reduce_over_line(normed, weights, ways)
+        outs = attend_part(
+            summed, cosine, sine, cache_key, cache_value, turn_len, cache_len, kv, kv_local, outs
+        )
+    return outs
 
 
 def local(*args):

time: 378 us -> 334 us (0.88)
  waiting for transfers between devices: 135 us -> 61.4 us
  local copies, waits for them, and re-layouts: 22.7 us -> 42.3 us
  matrix products: 25.8 us -> 38.1 us
  other arithmetic: 32 us -> 25.5 us
    ppermute x12, waiting for transfers between devices: 135 us -> 61.4 us  [the longest x4 48.7 us: reduce_over_line(): lax.ppermute(down.astype(jnp.bfloat16), 'wloop', [(ways - 1 - w, ways - 2...]
    dynamic_slice x0 -> x22, local copies, waits for them, and re-layouts: none -> 22.5 us  [pick(): lax.dynamic_index_in_dim(part, index, 0, keepdims=False)]
    dot_general x2 -> x8, matrix products: 25.8 us -> 38.1 us  [times(): jnp.einsum(spec, rows, w, preferred_element_type=jnp.float32)[..., kept]]
    squeeze x0 -> x1, local copies, waits for them, and re-layouts: none -> 10.6 us  [pick(): lax.dynamic_index_in_dim(part, index, 0, keepdims=False)]
    slice x4 -> x3, local copies, waits for them, and re-layouts: 9.89 us -> 1.98 us  [times(): jnp.einsum(spec, rows, w, preferred_element_type=jnp.float32)[..., kept]]
    convert_element_type x7 -> x9, other arithmetic: 23.5 us -> 16.9 us  [the longest x4 9.05 us: reduce_over_line(): down.astype(jnp.bfloat16)]
    convert_element_type x2 -> x0, local copies, waits for them, and re-layouts: 4.11 us -> none  [reduce_over_line(): up, down = (up.astype(jnp.bfloat16), down.astype(jnp.bfloat16))]
    unnamed x22 -> x74, local copies, waits for them, and re-layouts: 8.01 us -> 6.45 us
  transfers between devices with their start and end apart: 12 -> 12, of which waited for: 8 -> 8; matrix products, arithmetic and copies ran while one was open for 13% -> 28% of each run, Pallas kernels for 3% -> 3%
where the time goes in v4:
time: 334 us; the launch traced here: 332 us
  Pallas kernels  136 us (41%)
  waiting for transfers between devices  61.4 us (18%)
  local copies, waits for them, and re-layouts  42.3 us (13%)
  matrix products  38.1 us (11%)
  starting transfers between devices  28 us (8%)
  other arithmetic  25.5 us (8%)
    pallas_call x1, Pallas kernels, moved_normed(): pl.pallas_call(functools.partial(move_kernel, width), out_shape=jax.Shape...  113 us
    ppermute x4, waiting for transfers between devices, reduce_over_line(): lax.ppermute(down.astype(jnp.bfloat16), 'wloop', [(ways - 1 - w, ways - 2...  48.7 us
    dot_general x8, matrix products, times(): jnp.einsum(spec, rows, w, preferred_element_type=jnp.float32)[..., kept]  38.1 us
    pallas_call x2, Pallas kernels, attend_part(): pl.pallas_call(functools.partial(attend_kernel, q_cols // HEAD_DIM), grid...  23.1 us
    dynamic_slice x22, local copies, waits for them, and re-layouts, pick(): lax.dynamic_index_in_dim(part, index, 0, keepdims=False)  22.5 us
    ppermute x4, starting transfers between devices, reduce_over_line(): lax.ppermute(up.astype(jnp.bfloat16), 'wloop', [(w, w + 1) for w in range...  15.2 us
    ppermute x4, waiting for transfers between devices, reduce_over_line(): lax.ppermute(up.astype(jnp.bfloat16), 'wloop', [(w, w + 1) for w in range...  12.6 us
    squeeze x1, local copies, waits for them, and re-layouts, pick(): lax.dynamic_index_in_dim(part, index, 0, keepdims=False)  10.6 us
  transfers between devices with their start and end apart: 12, of which 8 were waited for; matrix products, arithmetic and copies ran while one was open for 28% of the time, Pallas kernels for 3%

profile of v4, /device:TPU:8, one launch (start us, length us, event | category | flops | bytes accessed | tf_op | source)
XLA Modules:
  0.0 332.3 jit_solution(4621145819904297917)
XLA Ops:
  1.4 1.6 copy-done.4
  3.0 112.7 %shard_map.112 = bf16[4,4,128,2048]{3,2,1,0:T(8,128)(2,1)S(1)} custom-call(bf16[512,2048]{1,0:T(8,128)(2,1)S(1)} %copy-done.4, f32[1,2048]{1,0:T(1,128)S(1)} %bitcast.87), custom_call_target="tpu_custom_call" | custom-call | tf_op jit(solution)/shard_map/pallas_call | solution.py:356
  116.5 1.3 copy-done.31
  118.5 2.8 slice-done.1
  121.3 2.3 fusion.26
  125.0 1.7 collective-permute-start.3
  128.0 2.3 fusion.31
  131.6 1.7 collective-permute-start.9
  133.3 1.5 collective-permute-start.6
  134.8 7.2 %fusion.46 = f32[4,512,256]{1,2,0:T(8,128)} fusion(bf16[4,512,2048]{2,1,0:T(8,128)(2,1)} %bitcast.83, bf16[2048,256]{1,0:T(8,128)(2,1)S(1)} %copy-done), kind=kOutput, calls=%fused_computation.56 | convolution fusion | flops 2147483648 | bytes 11534336 | tf_op jit(solution)/shard_map/brd,dn->brn/dot_general | solution.py:484
  142.0 2.4 fusion.48
  144.4 11.3 %fusion = f32[4,512,1024]{2,1,0:T(8,128)} fusion(bf16[4,512,2048]{2,1,0:T(8,128)(2,1)S(1)} %bitcast.85, bf16[2048,2048]{1,0:T(8,128)(2,1)S(1)} %bitcast.111), kind=kOutput, calls=%fused_computation | convolution fusion | flops 8589934592 | bytes 20971520 | tf_op jit(solution)/shard_map/brd,dn->brn/dot_general | solution.py:484
  155.7 11.1 %fusion.2 = f32[4,512,1024]{2,1,0:T(8,128)} fusion(bf16[4,512,2048]{2,1,0:T(8,128)(2,1)S(1)} %bitcast.86, bf16[2048,2048]{1,0:T(8,128)(2,1)S(1)} %bitcast.111), kind=kOutput, calls=%fused_computation.2 | convolution fusion | flops 8589934592 | bytes 20971520 | tf_op jit(solution)/shard_map/brd,dn->brn/dot_general | solution.py:484
  166.8 1.7 fusion.56
  168.6 1.5 constant_dynamic-slice_fusion.4
  170.0 1.8 copy.34
  171.9 1.8 copy.38
  173.7 1.8 copy.36
  175.4 1.8 copy.32
  177.2 1.8 copy.28
  184.9 10.6 %dynamic-slice_bitcast_fusion.2 = (f32[512,1024]{1,0:T(8,128)S(1)}, f32[512,1024]{1,0:T(8,128)}, f32[512,1024]{1,0:T(8,128)S(1)}, f32[512,1024]{1,0:T(8,128)S(1)...) fusion(f32[4,512,1024]{2,1,0:T(8,128)} %fusion, ...), kind=kLoop, calls=%fused_computation.38 | loop fusion | bytes 41943060 | tf_op jit(solution)/shard_map/jit(dynamic_index_in_dim)/squeeze | solution.py:500
  195.6 2.4 fusion.19
  198.0 1.5 collective-permute-start.10
  199.5 1.7 fusion.17
  201.3 4.6 %collective-permute-start.7 = (bf16[512,1280]{1,0:T(8,128)(2,1)S(1)}, bf16[512,1280]{1,0:T(8,128)(2,1)S(1)}, u32[]{:S(2)}, u32[]{:S(2)}) collective-permute-start(bf16[512,1280]{1,0:T(8,128)(2,1)S(1)} %fusion.17), channel_id=1, source_target_pairs={{0,4},{4,8},{1,5},{5,9},{2,6},{6,10},{3,7},{7,11},{16,20},{20,24},... | collective-permute-start | bytes 3932168 | tf_op jit(solution)/shard_map/ppermute | solution.py:506
  205.9 2.8 fusion.14
  210.0 2.8 fusion.12
  212.7 4.5 %collective-permute-start.1 = (bf16[512,1280]{1,0:T(8,128)(2,1)}, bf16[512,1280]{1,0:T(8,128)(2,1)}, u32[]{:S(2)}, u32[]{:S(2)}) collective-permute-start(bf16[512,1280]{1,0:T(8,128)(2,1)} %fusion.12), channel_id=1, source_target_pairs={{0,4},{4,8},{1,5},{5,9},{2,6},{6,10},{3,7},{7,11},{16,20},{20,24},... | collective-permute-start | bytes 3932168 | tf_op jit(solution)/shard_map/ppermute | solution.py:506
  217.3 14.2 %collective-permute-done.10 = bf16[512,1280]{1,0:T(8,128)(2,1)S(1)} collective-permute-done((bf16[512,1280]{1,0:T(8,128)(2,1)S(1)}, bf16[512,1280]{1,0:T(8,128)(2,1)S(1)}, u32[]{:S(2)}, u32[]{:S(2)}) %collective-permute-start.10) | collective-permute-done | bytes 1310752 | tf_op jit(solution)/shard_map/ppermute | solution.py:509
  231.5 1.5 fusion.18
  232.9 1.9 collective-permute-start.11
  234.9 1.7 collective-permute-done.7
  236.6 1.5 fusion.16
  238.1 2.9 collective-permute-start.8
  241.0 1.9 fusion.50
  249.4 1.4 pad_maximum_fusion.2
  250.8 8.9 %collective-permute-done.4 = bf16[512,1280]{1,0:T(8,128)(2,1)} collective-permute-done((bf16[512,1280]{1,0:T(8,128)(2,1)}, bf16[512,1280]{1,0:T(8,128)(2,1)}, u32[]{:S(2)}, u32[]{:S(2)}) %collective-permute-start.4) | collective-permute-done | bytes 1310752 | tf_op jit(solution)/shard_map/ppermute | solution.py:509
  259.7 2.4 fusion.13
  262.1 1.9 collective-permute-start.5
  264.8 1.9 fusion.11
  266.6 3.2 collective-permute-start.2
  269.9 17.9 %collective-permute-done.11 = bf16[512,1280]{1,0:T(8,128)(2,1)} collective-permute-done((bf16[512,1280]{1,0:T(8,128)(2,1)}, bf16[512,1280]{1,0:T(8,128)(2,1)}, u32[]{:S(2)}, u32[]{:S(2)}) %collective-permute-start.11) | collective-permute-done | bytes 1310752 | tf_op jit(solution)/shard_map/ppermute | solution.py:509
  287.7 5.1 %collective-permute-done.8 = bf16[512,1280]{1,0:T(8,128)(2,1)} collective-permute-done((bf16[512,1280]{1,0:T(8,128)(2,1)}, bf16[512,1280]{1,0:T(8,128)(2,1)}, u32[]{:S(2)}, u32[]{:S(2)}) %collective-permute-start.8) | collective-permute-done | bytes 1310752 | tf_op jit(solution)/shard_map/ppermute | solution.py:506
  292.9 2.3 fusion.15.q_ref.kv_ref
  295.9 11.5 %shard_map.113 = (bf16[512,2048]{1,0:T(8,128)(2,1)}, bf16[512,256]{1,0:T(8,128)(2,1)}, bf16[512,256]{1,0:T(8,128)(2,1)}) custom-call(s32[4]{0:T(128)S(1)} %copy-done.8, s32[4]{0:T(128)S(1)} %copy-done.5, f32[512,1280]{1,0:T(8,128)S(1)} %fusion.15.q_ref.kv_ref, f32[512,1280]{1,0:T(8,128)S(1)} %fusion.15.q_ref.kv_ref, ...), custom_call_target="tpu_custom_call" | custom-call | flops 9663676416 | bytes 10000000 | tf_op jit(solution)/shard_map/pallas_call | solution.py:455
  307.4 7.8 %collective-permute-done.5 = bf16[512,1280]{1,0:T(8,128)(2,1)S(1)} collective-permute-done((bf16[512,1280]{1,0:T(8,128)(2,1)S(1)}, bf16[512,1280]{1,0:T(8,128)(2,1)S(1)}, u32[]{:S(2)}, u32[]{:S(2)}) %collective-permute-start.5) | collective-permute-done | bytes 1310752 | tf_op jit(solution)/shard_map/ppermute | solution.py:509
  315.2 5.1 %collective-permute-done.2 = bf16[512,1280]{1,0:T(8,128)(2,1)S(1)} collective-permute-done((bf16[512,1280]{1,0:T(8,128)(2,1)S(1)}, bf16[512,1280]{1,0:T(8,128)(2,1)S(1)}, u32[]{:S(2)}, u32[]{:S(2)}) %collective-permute-start.2) | collective-permute-done | bytes 1310752 | tf_op jit(solution)/shard_map/ppermute | solution.py:506
  320.8 11.5 %shard_map.114 = (bf16[512,2048]{1,0:T(8,128)(2,1)}, bf16[512,256]{1,0:T(8,128)(2,1)}, bf16[512,256]{1,0:T(8,128)(2,1)}) custom-call(s32[4]{0:T(128)S(1)} %copy-done.8, s32[4]{0:T(128)S(1)} %copy-done.5, f32[512,1280]{1,0:T(8,128)S(1)} %fusion.10.q_ref.kv_ref, ...), custom_call_target="tpu_custom_call", output_to_operand_aliasing={{0}: (8, {}), {1}: (9, {}), {2}: (10, {})} | custom-call | flops 9663676416 | bytes 10000000 | tf_op jit(solution)/shard_map/pallas_call | solution.py:455
  (106 shorter events, 21.7 us)
Async XLA Ops:
  0.6 115.1 %copy-start = (bf16[2048,256]{1,0:T(8,128)(2,1)S(1)}, bf16[2048,256]{1,0:T(8,128)(2,1)}, u32[]{:S(2)}) copy-start(bf16[2048,256]{1,0:T(8,128)(2,1)} %param.13) | copy-start | bytes 3145732
  3.0 115.4 %slice-start = ((s8[8388608]{0:T(1024)(128)(4,1)}), s8[4194304]{0:T(1024)(128)(4,1)S(1)}, s32[]{:S(2)}) async-start(s8[8388608]{0:T(1024)(128)(4,1)} %bitcast.108), calls=%async_computation | async-start | bytes 8388608
  115.7 12.3 %copy-start.2 = (bf16[4,4,128,2048]{3,2,1,0:T(8,128)(2,1)}, bf16[4,4,128,2048]{3,2,1,0:T(8,128)(2,1)S(1)}, u32[]{:S(2)}) copy-start(bf16[4,4,128,2048]{3,2,1,0:T(8,128)(2,1)S(1)} %shard_map.112) | copy-start | bytes 25165828
  115.7 2.0 copy-start.31
  115.7 5.5 %slice-start.1 = ((s8[8388608]{0:T(1024)(128)(4,1)}), s8[4194304]{0:T(1024)(128)(4,1)S(1)}, s32[]{:S(2)}) async-start(s8[8388608]{0:T(1024)(128)(4,1)} %bitcast.108), calls=%async_computation.1 | async-start | bytes 8388608
  125.0 80.9 %collective-permute-start.3 = (bf16[512,1280]{1,0:T(8,128)(2,1)}, bf16[512,1280]{1,0:T(8,128)(2,1)}, u32[]{:S(2)}, u32[]{:S(2)}) collective-permute-start(bf16[512,1280]{1,0:T(8,128)(2,1)} %pad_maximum_fusion), channel_id=1, source_target_pairs={{12,8},{13,9},{14,10},{15,11},{28,24},{29,25},{30,26},{31,27}} | collective-permute-start | bytes 3932168 | tf_op jit(solution)/shard_map/ppermute | solution.py:494
  126.7 83.3 %collective-permute-start = (bf16[512,1280]{1,0:T(8,128)(2,1)}, bf16[512,1280]{1,0:T(8,128)(2,1)}, u32[]{:S(2)}, u32[]{:S(2)}) collective-permute-start(bf16[512,1280]{1,0:T(8,128)(2,1)} %pad_maximum_fusion), channel_id=1, source_target_pairs={{0,4},{1,5},{2,6},{3,7},{16,20},{17,21},{18,22},{19,23}} | collective-permute-start | bytes 3932168 | tf_op jit(solution)/shard_map/ppermute | solution.py:493
  131.6 64.0 %collective-permute-start.9 = (bf16[512,1280]{1,0:T(8,128)(2,1)}, bf16[512,1280]{1,0:T(8,128)(2,1)}, u32[]{:S(2)}, u32[]{:S(2)}) collective-permute-start(bf16[512,1280]{1,0:T(8,128)(2,1)} %pad_maximum_fusion.1), channel_id=1, source_target_pairs={{12,8},{13,9},{14,10},{15,11},{28,24},{29,25},{30,26},{31,27}} | collective-permute-start | bytes 3932168 | tf_op jit(solution)/shard_map/ppermute | solution.py:494
  133.3 66.2 %collective-permute-start.6 = (bf16[512,1280]{1,0:T(8,128)(2,1)}, bf16[512,1280]{1,0:T(8,128)(2,1)}, u32[]{:S(2)}, u32[]{:S(2)}) collective-permute-start(bf16[512,1280]{1,0:T(8,128)(2,1)} %pad_maximum_fusion.1), channel_id=1, source_target_pairs={{0,4},{1,5},{2,6},{3,7},{16,20},{17,21},{18,22},{19,23}} | collective-permute-start | bytes 3932168 | tf_op jit(solution)/shard_map/ppermute | solution.py:493
  134.8 7.3 %copy-start.3 = (bf16[4,4,128,2048]{3,2,1,0:T(8,128)(2,1)S(1)}, bf16[4,4,128,2048]{3,2,1,0:T(8,128)(2,1)}, u32[]{:S(2)}) copy-start(bf16[4,4,128,2048]{3,2,1,0:T(8,128)(2,1)} %copy-done.2) | copy-start | bytes 25165828
  134.8 7.3 %copy-start.32 = (bf16[2048,256]{1,0:T(8,128)(2,1)S(1)}, bf16[2048,256]{1,0:T(8,128)(2,1)}, u32[]{:S(2)}) copy-start(bf16[2048,256]{1,0:T(8,128)(2,1)} %param.12) | copy-start | bytes 3145732
  134.8 9.6 %slice-start.2 = ((s8[8388608]{0:T(1024)(128)(4,1)}), s8[4194304]{0:T(1024)(128)(4,1)S(1)}, s32[]{:S(2)}) async-start(s8[8388608]{0:T(1024)(128)(4,1)} %bitcast.110), calls=%async_computation.2 | async-start | bytes 8388608
  142.0 2.4 slice-start.3
  170.0 9.0 %copy-start.30 = (f32[1,512,128]{1,2,0:T(8,128)S(1)}, f32[1,512,128]{1,2,0:T(8,128)}, u32[]{:S(2)}) copy-start(f32[1,512,128]{1,2,0:T(8,128)} %get-tuple-element.54) | copy-start | bytes 786436
  184.8 10.6 %copy-start.5 = (s32[4]{0:T(128)S(1)}, s32[4]{0:T(128)}, u32[]{:S(2)}) copy-start(s32[4]{0:T(128)} %cache_len_ref.3) | copy-start | bytes 52
  184.9 10.7 %copy-start.23 = (f32[1,512,128]{2,1,0:T(8,128)S(1)}, f32[1,512,128]{2,1,0:T(8,128)}, u32[]{:S(2)}) copy-start(f32[1,512,128]{2,1,0:T(8,128)} %copy.38) | copy-start | bytes 786436
  184.9 10.7 %copy-start.28 = (f32[1,512,128]{2,1,0:T(8,128)S(1)}, f32[1,512,128]{2,1,0:T(8,128)}, u32[]{:S(2)}) copy-start(f32[1,512,128]{2,1,0:T(8,128)} %copy.37) | copy-start | bytes 786436
  195.6 3.9 %copy-start.21 = (f32[1,512,128]{2,1,0:T(8,128)S(1)}, f32[1,512,128]{2,1,0:T(8,128)}, u32[]{:S(2)}) copy-start(f32[1,512,128]{2,1,0:T(8,128)} %copy.34) | copy-start | bytes 786436
  195.6 3.9 %copy-start.26 = (f32[1,512,128]{2,1,0:T(8,128)S(1)}, f32[1,512,128]{2,1,0:T(8,128)}, u32[]{:S(2)}) copy-start(f32[1,512,128]{2,1,0:T(8,128)} %copy.33) | copy-start | bytes 786436
  198.0 33.5 %collective-permute-start.10 = (bf16[512,1280]{1,0:T(8,128)(2,1)S(1)}, bf16[512,1280]{1,0:T(8,128)(2,1)S(1)}, u32[]{:S(2)}, u32[]{:S(2)}) collective-permute-start(bf16[512,1280]{1,0:T(8,128)(2,1)S(1)} %fusion.19), channel_id=1, source_target_pairs={{12,8},{8,4},{13,9},{9,5},{14,10},{10,6},{15,11},{11,7},{28,24},{2... | collective-permute-start | bytes 3932168 | tf_op jit(solution)/shard_map/ppermute | solution.py:509
  199.5 6.3 %copy-start.20 = (f32[1,512,128]{2,1,0:T(8,128)S(1)}, f32[1,512,128]{2,1,0:T(8,128)}, u32[]{:S(2)}) copy-start(f32[1,512,128]{2,1,0:T(8,128)} %copy.28) | copy-start | bytes 786436
  199.5 6.3 %copy-start.25 = (f32[1,512,128]{2,1,0:T(8,128)S(1)}, f32[1,512,128]{2,1,0:T(8,128)}, u32[]{:S(2)}) copy-start(f32[1,512,128]{2,1,0:T(8,128)} %copy.27) | copy-start | bytes 786436
  201.3 35.3 %collective-permute-start.7 = (bf16[512,1280]{1,0:T(8,128)(2,1)S(1)}, bf16[512,1280]{1,0:T(8,128)(2,1)S(1)}, u32[]{:S(2)}, u32[]{:S(2)}) collective-permute-start(bf16[512,1280]{1,0:T(8,128)(2,1)S(1)} %fusion.17), channel_id=1, source_target_pairs={{0,4},{4,8},{1,5},{5,9},{2,6},{6,10},{3,7},{7,11},{16,20},{20,24},... | collective-permute-start | bytes 3932168 | tf_op jit(solution)/shard_map/ppermute | solution.py:506
  205.9 4.1 %copy-start.18 = (f32[1,512,128]{2,1,0:T(8,128)S(1)}, f32[1,512,128]{2,1,0:T(8,128)}, u32[]{:S(2)}) copy-start(f32[1,512,128]{2,1,0:T(8,128)} %copy.22) | copy-start | bytes 786436
  208.6 51.0 %collective-permute-start.4 = (bf16[512,1280]{1,0:T(8,128)(2,1)}, bf16[512,1280]{1,0:T(8,128)(2,1)}, u32[]{:S(2)}, u32[]{:S(2)}) collective-permute-start(bf16[512,1280]{1,0:T(8,128)(2,1)} %fusion.14), channel_id=1, source_target_pairs={{12,8},{8,4},{13,9},{9,5},{14,10},{10,6},{15,11},{11,7},{28,24},{2... | collective-permute-start | bytes 3932168 | tf_op jit(solution)/shard_map/ppermute | solution.py:509
  209.9 21.5 %copy-start.17 = (f32[1,512,128]{2,1,0:T(8,128)S(1)}, f32[1,512,128]{2,1,0:T(8,128)}, u32[]{:S(2)}) copy-start(f32[1,512,128]{2,1,0:T(8,128)} %copy.36) | copy-start | bytes 786436
  212.7 52.0 %collective-permute-start.1 = (bf16[512,1280]{1,0:T(8,128)(2,1)}, bf16[512,1280]{1,0:T(8,128)(2,1)}, u32[]{:S(2)}, u32[]{:S(2)}) collective-permute-start(bf16[512,1280]{1,0:T(8,128)(2,1)} %fusion.12), channel_id=1, source_target_pairs={{0,4},{4,8},{1,5},{5,9},{2,6},{6,10},{3,7},{7,11},{16,20},{20,24},... | collective-permute-start | bytes 3932168 | tf_op jit(solution)/shard_map/ppermute | solution.py:506
  231.5 5.1 %copy-start.16 = (f32[1,512,128]{2,1,0:T(8,128)S(1)}, f32[1,512,128]{2,1,0:T(8,128)}, u32[]{:S(2)}) copy-start(f32[1,512,128]{2,1,0:T(8,128)} %copy.32) | copy-start | bytes 786436
  231.5 5.1 %copy-start.19 = (f32[1,512,128]{2,1,0:T(8,128)S(1)}, f32[1,512,128]{2,1,0:T(8,128)}, u32[]{:S(2)}) copy-start(f32[1,512,128]{2,1,0:T(8,128)} %copy.31) | copy-start | bytes 786436
  232.9 54.8 %collective-permute-start.11 = (bf16[512,1280]{1,0:T(8,128)(2,1)}, bf16[512,1280]{1,0:T(8,128)(2,1)}, u32[]{:S(2)}, u32[]{:S(2)}) collective-permute-start(bf16[512,1280]{1,0:T(8,128)(2,1)} %fusion.18), channel_id=1, source_target_pairs={{12,8},{8,4},{4,0},{13,9},{9,5},{5,1},{14,10},{10,6},{6,2},{15,11}... | collective-permute-start | bytes 3932168 | tf_op jit(solution)/shard_map/ppermute | solution.py:509
  236.6 6.3 %copy-start.13 = (f32[1,512,128]{1,2,0:T(8,128)S(1)}, f32[1,512,128]{1,2,0:T(8,128)}, u32[]{:S(2)}) copy-start(f32[1,512,128]{1,2,0:T(8,128)} %get-tuple-element.32) | copy-start | bytes 786436
  236.6 7.1 %copy-start.12 = (f32[1,512,128]{1,2,0:T(8,128)S(1)}, f32[1,512,128]{1,2,0:T(8,128)}, u32[]{:S(2)}) copy-start(f32[1,512,128]{1,2,0:T(8,128)} %get-tuple-element.50) | copy-start | bytes 786436
  236.6 8.0 %copy-start.11 = (f32[1,512,128]{1,2,0:T(8,128)S(1)}, f32[1,512,128]{1,2,0:T(8,128)}, u32[]{:S(2)}) copy-start(f32[1,512,128]{1,2,0:T(8,128)} %get-tuple-element.51) | copy-start | bytes 786436
  238.1 10.5 %copy-start.14 = (f32[1,512,128]{1,2,0:T(8,128)S(1)}, f32[1,512,128]{1,2,0:T(8,128)}, u32[]{:S(2)}) copy-start(f32[1,512,128]{1,2,0:T(8,128)} %get-tuple-element.62) | copy-start | bytes 786436
  238.1 54.8 %collective-permute-start.8 = (bf16[512,1280]{1,0:T(8,128)(2,1)}, bf16[512,1280]{1,0:T(8,128)(2,1)}, u32[]{:S(2)}, u32[]{:S(2)}) collective-permute-start(bf16[512,1280]{1,0:T(8,128)(2,1)} %fusion.16), channel_id=1, source_target_pairs={{0,4},{4,8},{8,12},{1,5},{5,9},{9,13},{2,6},{6,10},{10,14},{3,7},{... | collective-permute-start | bytes 3932168 | tf_op jit(solution)/shard_map/ppermute | solution.py:506
  243.7 4.0 %copy-start.15 = (f32[1,512,128]{1,2,0:T(8,128)S(1)}, f32[1,512,128]{1,2,0:T(8,128)}, u32[]{:S(2)}) copy-start(f32[1,512,128]{1,2,0:T(8,128)} %get-tuple-element.61) | copy-start | bytes 786436
  259.6 5.1 %copy-start.27 = (f32[1,512,128]{2,1,0:T(8,128)S(1)}, f32[1,512,128]{2,1,0:T(8,128)}, u32[]{:S(2)}) copy-start(f32[1,512,128]{2,1,0:T(8,128)} %copy.20) | copy-start | bytes 786436
  259.6 5.1 %copy-start.29 = (f32[1,512,128]{2,1,0:T(8,128)S(1)}, f32[1,512,128]{2,1,0:T(8,128)}, u32[]{:S(2)}) copy-start(f32[1,512,128]{2,1,0:T(8,128)} %copy.19) | copy-start | bytes 786436
  262.1 53.1 %collective-permute-start.5 = (bf16[512,1280]{1,0:T(8,128)(2,1)S(1)}, bf16[512,1280]{1,0:T(8,128)(2,1)S(1)}, u32[]{:S(2)}, u32[]{:S(2)}) collective-permute-start(bf16[512,1280]{1,0:T(8,128)(2,1)S(1)} %fusion.13), channel_id=1, source_target_pairs={{12,8},{8,4},{4,0},{13,9},{9,5},{5,1},{14,10},{10,6},{6,2},{15,11}... | collective-permute-start | bytes 3932168 | tf_op jit(solution)/shard_map/ppermute | solution.py:509
  264.8 28.1 %copy-start.10 = (f32[512,1024]{1,0:T(8,128)S(1)}, f32[512,1024]{1,0:T(8,128)}, u32[]{:S(2)}) copy-start(f32[512,1024]{1,0:T(8,128)} %get-tuple-element.13) | copy-start | bytes 6291460
  264.8 28.1 %copy-start.24 = (f32[1,512,128]{2,1,0:T(8,128)S(1)}, f32[1,512,128]{2,1,0:T(8,128)}, u32[]{:S(2)}) copy-start(f32[1,512,128]{2,1,0:T(8,128)} %copy.30) | copy-start | bytes 786436
  266.6 53.6 %collective-permute-start.2 = (bf16[512,1280]{1,0:T(8,128)(2,1)S(1)}, bf16[512,1280]{1,0:T(8,128)(2,1)S(1)}, u32[]{:S(2)}, u32[]{:S(2)}) collective-permute-start(bf16[512,1280]{1,0:T(8,128)(2,1)S(1)} %fusion.11), channel_id=1, source_target_pairs={{0,4},{4,8},{8,12},{1,5},{5,9},{9,13},{2,6},{6,10},{10,14},{3,7},{... | collective-permute-start | bytes 3932168 | tf_op jit(solution)/shard_map/ppermute | solution.py:506
  292.8 2.4 copy-start.6
  292.8 3.0 copy-start.7
  292.9 3.0 copy-start.8
  295.9 24.4 %copy-start.9 = (f32[512,1024]{1,0:T(8,128)S(1)}, f32[512,1024]{1,0:T(8,128)}, u32[]{:S(2)}) copy-start(f32[512,1024]{1,0:T(8,128)} %get-tuple-element.55) | copy-start | bytes 6291460
  295.9 24.4 %copy-start.22 = (f32[1,512,128]{2,1,0:T(8,128)S(1)}, f32[1,512,128]{2,1,0:T(8,128)}, u32[]{:S(2)}) copy-start(f32[1,512,128]{2,1,0:T(8,128)} %copy.18) | copy-start | bytes 786436
  320.7 11.5 %copy-start.1 = (bf16[2048,256]{1,0:T(8,128)(2,1)S(1)}, bf16[2048,256]{1,0:T(8,128)(2,1)}, u32[]{:S(2)}) copy-start(bf16[2048,256]{1,0:T(8,128)(2,1)} %param.13) | copy-start | bytes 3145732
  (1 other events, 1.6 us)
